TPU v7x, 32 devices: a whole 2x2x4 slice. The times are simulated.
32 devices in a mesh: dp: 8 (over y, x, core), row: 4 (over z).
Axes of the slice: x: 2, y: 2, z: 4, core: 2. Of those that a mesh axis runs over, the one named last changes fastest.
Arguments:
- latent: bfloat16 [64, 12, 12, 256], P('dp', 'row'), may hold values from -6 to 6
- codes: int32 [64, 12, 12], P('dp', 'row'), may hold values from 0 to 16383
- codebook: bfloat16 [16384, 256], P('row'), may hold values from -6 to 6
- post_weight: bfloat16 [256, 256], replicated, may hold values from -0.375 to 0.375
- post_bias: float32 [256], replicated, may hold values from -3 to 3
- entry_weight: bfloat16 [9, 256, 512], replicated, may hold values from -0.125 to 0.125
- entry_bias: float32 [512], replicated, may hold values from -3 to 3
- first_gain: float32 [512], replicated, may hold values from 0.25 to 1.75
- first_shift: float32 [512], replicated, may hold values from -3 to 3
- first_weight: bfloat16 [9, 512, 512], replicated, may hold values from -0.09375 to 0.09375
- first_bias: float32 [512], replicated, may hold values from -3 to 3
- second_gain: float32 [512], replicated, may hold values from 0.25 to 1.75
- second_shift: float32 [512], replicated, may hold values from -3 to 3
- second_weight: bfloat16 [9, 512, 512], replicated, may hold values from -0.09375 to 0.09375
- second_bias: float32 [512], replicated, may hold values from -3 to 3
- mixer_gain: float32 [512], replicated, may hold values from 0.25 to 1.75
- mixer_shift: float32 [512], replicated, may hold values from -3 to 3
- query_weight: bfloat16 [512, 512], replicated, may hold values from -0.25 to 0.25
- query_bias: float32 [512], replicated, may hold values from -3 to 3
- key_weight: bfloat16 [512, 512], replicated, may hold values from -0.25 to 0.25
- value_weight: bfloat16 [512, 512], replicated, may hold values from -0.25 to 0.25
- value_bias: float32 [512], replicated, may hold values from -3 to 3
- projection_output_weight: bfloat16 [512, 512], replicated, may hold values from -1.5 to 1.5
- projection_output_bias: float32 [512], replicated, may hold values from -3 to 3
- cotangent: bfloat16 [64, 12, 12, 512], P('dp', 'row'), may hold values from -6 to 6
Outputs:
- decoded: bfloat16 [64, 12, 12, 512], P('dp', 'row')
- latent_grad: float32 [64, 12, 12, 256], P('dp', 'row')
- codebook_grad: float32 [16384, 256], P(('row', 'dp'))
- post_weight_grad: float32 [256, 256], P('dp')
- post_bias_grad: float32 [256], P('dp')
- entry_weight_grad: float32 [9, 256, 512], P(None, 'dp')
- entry_bias_grad: float32 [512], P('dp')
- first_gain_grad: float32 [512], P('dp')
- first_shift_grad: float32 [512], P('dp')
- first_weight_grad: float32 [9, 512, 512], P(None, 'dp')
- first_bias_grad: float32 [512], P('dp')
- second_gain_grad: float32 [512], P('dp')
- second_shift_grad: float32 [512], P('dp')
- second_weight_grad: float32 [9, 512, 512], P(None, 'dp')
- second_bias_grad: float32 [512], P('dp')
- mixer_gain_grad: float32 [512], P('dp')
- mixer_shift_grad: float32 [512], P('dp')
- query_weight_grad: float32 [512, 512], P('dp')
- query_bias_grad: float32 [512], P('dp')
- key_weight_grad: float32 [512, 512], P('dp')
- value_weight_grad: float32 [512, 512], P('dp')
- value_bias_grad: float32 [512], P('dp')
- output_weight_grad: float32 [512, 512], P('dp')
- output_bias_grad: float32 [512], P('dp')
Inputs may be any that keep to these rules, and one draw needn't show every extreme that they name: `codes`: one code index for every latent position.
All inputs are finite; a program needn't handle non-finite values.
Results may differ from a plain program's by a relative error of at most 0.023.
Values may be sent and summed in bfloat16 or wider, within the bound.
No kernel may reach another device: no remote copies, remote signals or barrier semaphores. Data moves between devices by JAX's collectives and lax.ppermute only.
A program may use at most 128 MiB of HBM per device.

v0:
```python
import jax
import jax.numpy as jnp
from jax import lax
from jax.sharding import PartitionSpec as P

GROUPS = 32


EPSILON = 1e-06
BETA_COMMIT = 0.25


def padded_2(cells, sides, width):
    for axis, dim in sides:
        count = lax.axis_size(axis)
        ends = count - 1
        head = lax.slice_in_dim(cells, 0, width, axis=dim)
        tail = lax.slice_in_dim(cells, cells.shape[dim] - width, cells.shape[dim], axis=dim)
        cells = jnp.concatenate(
            [
                lax.ppermute(tail, axis, [(i, (i + 1) % count) for i in range(ends)]),
                cells,
                lax.ppermute(head, axis, [((i + 1) % count, i) for i in range(ends)]),
            ],
            axis=dim,
        )
    return cells


def bfloat(tensor):
    return tensor.astype(jnp.bfloat16)


def pad_columns(tensor):
    return jnp.pad(tensor, ((0, 0), (0, 0), (1, 1), (0, 0)))


def add_rims(tensor):
    padded = padded_2(tensor, (("row", 1),), 1)
    return pad_columns(padded)


def add_grad_rims(tensor):
    padded = padded_2(tensor, (("row", 1),), 1)
    return pad_columns(padded)


def patches(padded, reverse):
    rows_local = padded.shape[1] - 2
    cols_local = padded.shape[2] - 2
    tap_list = []
    for row_tap in range(3):
        for col_tap in range(3):
            row_start = 2 - row_tap if reverse else row_tap
            col_start = 2 - col_tap if reverse else col_tap
            tap_list.append(
                padded[:, row_start : row_start + rows_local, col_start : col_start + cols_local, :]
            )
    return jnp.stack(tap_list, axis=3)


def conv_apply(columns, kernel):
    return jnp.einsum("bhwtc,tcf->bhwf", columns, kernel, preferred_element_type=jnp.float32)


def conv_back(columns, kernel):
    return jnp.einsum("bhwtf,tcf->bhwc", columns, kernel, preferred_element_type=jnp.float32)


def kernel_grad(columns, gradient):
    return jnp.einsum("bhwtc,bhwf->tcf", columns, gradient, preferred_element_type=jnp.float32)


def group_view(tensor):
    batch_size, rows_local, cols_local, channel_count = tensor.shape
    return tensor.reshape(batch_size, rows_local * cols_local, GROUPS, channel_count // GROUPS)


def member_count(tensor):
    spread = lax.axis_size("row")
    return tensor.shape[1] * tensor.shape[2] * spread * (tensor.shape[3] // GROUPS)


def group_stats(tensor):
    grouped = group_view(tensor)
    first_sum = jnp.sum(grouped, axis=(1, 3))
    second_sum = jnp.sum(grouped * grouped, axis=(1, 3))
    first_sum, second_sum = lax.psum((first_sum, second_sum), "row")
    members = member_count(tensor)
    average = first_sum / members
    variance = second_sum / members - average * average
    return (average, lax.rsqrt(variance + EPSILON))


def normalize(tensor, average, inverse):
    grouped = group_view(tensor)
    scaled = (grouped - average[:, None, :, None]) * inverse[:, None, :, None]
    return scaled.reshape(tensor.shape)


def norm_back(gradient, standard, inverse, gain_vec):
    gain_grad = jnp.sum(gradient * standard, axis=(0, 1, 2))
    shift_grad = jnp.sum(gradient, axis=(0, 1, 2))
    scaled = group_view(gradient * gain_vec)
    normal = group_view(standard)
    first_sum = jnp.sum(scaled, axis=(1, 3))
    second_sum = jnp.sum(scaled * normal, axis=(1, 3))
    first_sum, second_sum = lax.psum((first_sum, second_sum), "row")
    members = member_count(gradient)
    final_output = (
        scaled
        - (first_sum / members)[:, None, :, None]
        - normal * (second_sum / members)[:, None, :, None]
    ) * inverse[:, None, :, None]
    return (final_output.reshape(gradient.shape), gain_grad, shift_grad)


def silu_slope(pre_act):
    logistic = jax.nn.sigmoid(pre_act)
    return logistic * (1.0 + pre_act * (1.0 - logistic))


def activate(tensor, average, inverse, gain_vec, shift_vec):
    standard = normalize(tensor, average, inverse)
    pre_act = standard * gain_vec + shift_vec
    columns = patches(add_rims(bfloat(jax.nn.silu(pre_act))), False)
    return (standard, pre_act, columns)


def to_images(tensor):
    return lax.all_to_all(tensor, "row", split_axis=0, concat_axis=1, tiled=True)


def to_rows(tensor):
    return lax.all_to_all(tensor, "row", split_axis=1, concat_axis=0, tiled=True)


def on_device(
    latent,
    codes,
    codebook,
    post_weight,
    post_bias,
    entry_weight,
    entry_bias,
    first_gain,
    first_shift,
    first_weight,
    first_bias,
    second_gain,
    second_shift,
    second_weight,
    second_bias,
    mixer_gain,
    mixer_shift,
    query_weight,
    query_bias,
    key_weight,
    value_weight,
    value_bias,
    projection_output_weight,
    projection_output_bias,
    cotangent,
):
    batch_size, rows_local, cols_local, embed_dim = latent.shape
    channel_count = entry_weight.shape[2]
    row_count = lax.axis_size("row")
    owned_rows = codebook.shape[0]
    positions = batch_size * rows_local * cols_local
    all_codes = lax.all_gather(codes, "row", axis=1, tiled=True)
    code_order = (
        all_codes.reshape(batch_size, row_count, rows_local, cols_local)
        .transpose(1, 0, 2, 3)
        .reshape(row_count * positions)
    )
    first_code = lax.axis_index("row") * owned_rows
    whole_book = lax.all_gather(codebook, "row", axis=0, tiled=True)
    local_codes = codes.reshape(positions)
    one_hot = (
        local_codes[:, None] == lax.broadcasted_iota(jnp.int32, (positions, whole_book.shape[0]), 1)
    ).astype(jnp.bfloat16)
    looked = jnp.dot(one_hot, whole_book, preferred_element_type=jnp.float32)
    quant_flat = bfloat(looked)
    quant_grid = quant_flat.reshape(latent.shape)
    quant_work, cot_work = (quant_grid, cotangent)
    work_batch, work_rows = (quant_work.shape[0], quant_work.shape[1])
    work_positions = work_batch * work_rows * cols_local
    quant_work_flat = quant_work.reshape(work_positions, embed_dim)
    post = jnp.dot(quant_work_flat, post_weight, preferred_element_type=jnp.float32) + post_bias
    post_low = bfloat(post).reshape(work_batch, work_rows, cols_local, embed_dim)
    post_cols = patches(add_rims(post_low), False)
    stream = conv_apply(post_cols, entry_weight) + entry_bias
    average_one, inverse_one = group_stats(stream)
    standard_one, pre_one, cols_one = activate(
        stream, average_one, inverse_one, first_gain, first_shift
    )
    middle = conv_apply(cols_one, first_weight) + first_bias
    average_two, inverse_two = group_stats(middle)
    standard_two, pre_two, cols_two = activate(
        middle, average_two, inverse_two, second_gain, second_shift
    )
    hidden = stream + (conv_apply(cols_two, second_weight) + second_bias)
    average_mix, inverse_mix = group_stats(hidden)
    standard_mix = normalize(hidden, average_mix, inverse_mix)
    images = to_images(bfloat(standard_mix * mixer_gain + mixer_shift))
    image_count, rows_total = (images.shape[0], images.shape[1])
    sequence = rows_total * cols_local
    tokens = images.reshape(image_count, sequence, channel_count)
    query_rows = bfloat(
        jnp.einsum("bsc,cd->bsd", tokens, query_weight, preferred_element_type=jnp.float32)
        + query_bias
    )
    key_matrix_rows = bfloat(
        jnp.einsum("bsc,cd->bsd", tokens, key_weight, preferred_element_type=jnp.float32)
    )
    value_matrix_rows = bfloat(
        jnp.einsum("bsc,cd->bsd", tokens, value_weight, preferred_element_type=jnp.float32)
        + value_bias
    )
    score_scale = channel_count ** (-0.5)
    attention_logits = (
        jnp.einsum("nsw,nlw->nsl", query_rows, key_matrix_rows, preferred_element_type=jnp.float32)
        * score_scale
    )
    peak = jnp.max(attention_logits, axis=2, keepdims=True)
    exponents = jnp.exp(attention_logits - peak)
    totals = jnp.sum(exponents, axis=2, keepdims=True)
    attention_probs_reduced = bfloat(exponents / totals)
    log_total = peak + jnp.log(totals)
    attention_output = bfloat(
        jnp.einsum(
            "lah,lhy->lay",
            attention_probs_reduced,
            value_matrix_rows,
            preferred_element_type=jnp.float32,
        )
    )
    final_output = bfloat(
        jnp.einsum(
            "pzn,nt->pzt",
            attention_output,
            projection_output_weight,
            preferred_element_type=jnp.float32,
        )
        + projection_output_bias
    )
    returned = to_rows(final_output.reshape(image_count, rows_total, cols_local, channel_count))
    decoded_work = bfloat(hidden + returned.astype(jnp.float32))
    grad_output = cot_work.astype(jnp.float32)
    picture_gradient = to_images(cot_work).reshape(image_count, sequence, channel_count)
    grad_output_weight = jnp.einsum(
        "fwt,fwx->tx", attention_output, picture_gradient, preferred_element_type=jnp.float32
    )
    grad_output_bias = jnp.sum(picture_gradient.astype(jnp.float32), axis=(0, 1))
    attention_output_gradient = bfloat(
        jnp.einsum(
            "oju,iu->oji",
            picture_gradient,
            projection_output_weight,
            preferred_element_type=jnp.float32,
        )
    )
    grad_weights = jnp.einsum(
        "nsw,nlw->nsl",
        attention_output_gradient,
        value_matrix_rows,
        preferred_element_type=jnp.float32,
    )
    grad_values = bfloat(
        jnp.einsum(
            "xzv,xzj->xvj",
            attention_probs_reduced,
            attention_output_gradient,
            preferred_element_type=jnp.float32,
        )
    )
    repeat_pass = (
        jnp.einsum("nsw,nlw->nsl", query_rows, key_matrix_rows, preferred_element_type=jnp.float32)
        * score_scale
    )
    probs = jnp.exp(repeat_pass - log_total)
    score_gradient = bfloat(
        probs * (grad_weights - jnp.sum(grad_weights * probs, axis=2, keepdims=True))
    )
    grad_query = bfloat(
        jnp.einsum(
            "lah,lhy->lay", score_gradient, key_matrix_rows, preferred_element_type=jnp.float32
        )
        * score_scale
    )
    grad_keys = bfloat(
        jnp.einsum("xzv,xzj->xvj", score_gradient, query_rows, preferred_element_type=jnp.float32)
        * score_scale
    )
    grad_query_weight = jnp.einsum(
        "bsc,bsd->cd", tokens, grad_query, preferred_element_type=jnp.float32
    )
    grad_query_bias = jnp.sum(grad_query.astype(jnp.float32), axis=(0, 1))
    grad_key_weight = jnp.einsum(
        "bsc,bsd->cd", tokens, grad_keys, preferred_element_type=jnp.float32
    )
    grad_value_weight = jnp.einsum(
        "bsc,bsd->cd", tokens, grad_values, preferred_element_type=jnp.float32
    )
    grad_value_bias = jnp.sum(grad_values.astype(jnp.float32), axis=(0, 1))
    grad_tokens = (
        jnp.einsum("bsd,cd->bsc", grad_query, query_weight, preferred_element_type=jnp.float32)
        + jnp.einsum("bsd,cd->bsc", grad_keys, key_weight, preferred_element_type=jnp.float32)
        + jnp.einsum("bsd,cd->bsc", grad_values, value_weight, preferred_element_type=jnp.float32)
    )
    grad_normed = to_rows(
        bfloat(grad_tokens).reshape(image_count, rows_total, cols_local, channel_count)
    ).astype(jnp.float32)
    grad_mix_in, grad_mixer_gain, grad_mixer_shift = norm_back(
        grad_normed, standard_mix, inverse_mix, mixer_gain
    )
    grad_hidden = grad_output + grad_mix_in
    standard_one, pre_one, cols_one = activate(
        stream, average_one, inverse_one, first_gain, first_shift
    )
    middle = conv_apply(cols_one, first_weight) + first_bias
    standard_two, pre_two, cols_two = activate(
        middle, average_two, inverse_two, second_gain, second_shift
    )
    grad_branch = bfloat(grad_hidden)
    grad_second_weight = kernel_grad(cols_two, grad_branch)
    grad_second_bias = jnp.sum(grad_branch.astype(jnp.float32), axis=(0, 1, 2))
    grad_act_two = conv_back(patches(add_grad_rims(grad_branch), True), second_weight)
    grad_middle_full, grad_second_gain, grad_second_shift = norm_back(
        grad_act_two * silu_slope(pre_two), standard_two, inverse_two, second_gain
    )
    grad_middle = bfloat(grad_middle_full)
    grad_first_weight = kernel_grad(cols_one, grad_middle)
    grad_first_bias = jnp.sum(grad_middle.astype(jnp.float32), axis=(0, 1, 2))
    grad_act_one = conv_back(patches(add_grad_rims(grad_middle), True), first_weight)
    grad_stream_norm, grad_first_gain, grad_first_shift = norm_back(
        grad_act_one * silu_slope(pre_one), standard_one, inverse_one, first_gain
    )
    grad_stream = bfloat(grad_hidden + grad_stream_norm)
    grad_entry_weight = kernel_grad(post_cols, grad_stream)
    grad_entry_bias = jnp.sum(grad_stream.astype(jnp.float32), axis=(0, 1, 2))
    grad_post = bfloat(conv_back(patches(add_grad_rims(grad_stream), True), entry_weight)).reshape(
        work_positions, embed_dim
    )
    grad_post_weight = jnp.einsum(
        "pe,pf->ef", quant_work_flat, grad_post, preferred_element_type=jnp.float32
    )
    grad_post_bias = jnp.sum(grad_post.astype(jnp.float32), axis=0)
    grad_quant_work = jnp.einsum(
        "pf,ef->pe", grad_post, post_weight, preferred_element_type=jnp.float32
    )
    grad_quant_work = grad_quant_work.reshape(work_batch, work_rows, cols_local, embed_dim)
    decoded, grad_quant = (decoded_work, grad_quant_work)
    latent_float = latent.astype(jnp.float32)
    quant_float = quant_grid.astype(jnp.float32)
    latent_grad = grad_quant + 2.0 * BETA_COMMIT * (latent_float - quant_float)
    difference = bfloat(2.0 * (quant_float - latent_float)).reshape(positions, embed_dim)
    portion = lax.all_gather(difference, "row", axis=0, tiled=True)
    one_hot = (
        code_order[:, None] - first_code
        == lax.broadcasted_iota(jnp.int32, (portion.shape[0], owned_rows), 1)
    ).astype(jnp.bfloat16)
    grad_book = jnp.einsum("pk,pe->ke", one_hot, portion, preferred_element_type=jnp.float32)
    (
        share_post_weight,
        share_post_bias,
        share_entry_weight,
        share_entry_bias,
        share_first_gain,
        share_first_shift,
        share_first_weight,
        share_first_bias,
        share_second_gain,
        share_second_shift,
        share_second_weight,
        share_second_bias,
        codebook_grad,
        share_mixer_gain,
        share_mixer_shift,
        share_query_weight,
        share_query_bias,
        share_key_weight,
        share_value_weight,
        share_value_bias,
        share_output_weight,
        share_output_bias,
    ) = (
        lax.psum_scatter(grad_post_weight, "dp", scatter_dimension=0, tiled=True),
        lax.psum_scatter(grad_post_bias, "dp", scatter_dimension=0, tiled=True),
        lax.psum_scatter(grad_entry_weight, "dp", scatter_dimension=1, tiled=True),
        lax.psum_scatter(grad_entry_bias, "dp", scatter_dimension=0, tiled=True),
        lax.psum_scatter(grad_first_gain, "dp", scatter_dimension=0, tiled=True),
        lax.psum_scatter(grad_first_shift, "dp", scatter_dimension=0, tiled=True),
        lax.psum_scatter(grad_first_weight, "dp", scatter_dimension=1, tiled=True),
        lax.psum_scatter(grad_first_bias, "dp", scatter_dimension=0, tiled=True),
        lax.psum_scatter(grad_second_gain, "dp", scatter_dimension=0, tiled=True),
        lax.psum_scatter(grad_second_shift, "dp", scatter_dimension=0, tiled=True),
        lax.psum_scatter(grad_second_weight, "dp", scatter_dimension=1, tiled=True),
        lax.psum_scatter(grad_second_bias, "dp", scatter_dimension=0, tiled=True),
        lax.psum_scatter(grad_book, "dp", scatter_dimension=0, tiled=True),
        lax.psum_scatter(grad_mixer_gain, "dp", scatter_dimension=0, tiled=True),
        lax.psum_scatter(grad_mixer_shift, "dp", scatter_dimension=0, tiled=True),
        lax.psum_scatter(grad_query_weight, "dp", scatter_dimension=0, tiled=True),
        lax.psum_scatter(grad_query_bias, "dp", scatter_dimension=0, tiled=True),
        lax.psum_scatter(grad_key_weight, "dp", scatter_dimension=0, tiled=True),
        lax.psum_scatter(grad_value_weight, "dp", scatter_dimension=0, tiled=True),
        lax.psum_scatter(grad_value_bias, "dp", scatter_dimension=0, tiled=True),
        lax.psum_scatter(grad_output_weight, "dp", scatter_dimension=0, tiled=True),
        lax.psum_scatter(grad_output_bias, "dp", scatter_dimension=0, tiled=True),
    )
    summed = (
        lax.psum(share_post_weight.astype(jnp.bfloat16), "row").astype(jnp.float32),
        lax.psum(share_post_bias.astype(jnp.bfloat16), "row").astype(jnp.float32),
        lax.psum(share_entry_weight.astype(jnp.bfloat16), "row").astype(jnp.float32),
        lax.psum(share_entry_bias.astype(jnp.bfloat16), "row").astype(jnp.float32),
        lax.psum(share_first_gain.astype(jnp.bfloat16), "row").astype(jnp.float32),
        lax.psum(share_first_shift.astype(jnp.bfloat16), "row").astype(jnp.float32),
        lax.psum(share_first_weight.astype(jnp.bfloat16), "row").astype(jnp.float32),
        lax.psum(share_first_bias.astype(jnp.bfloat16), "row").astype(jnp.float32),
        lax.psum(share_second_gain.astype(jnp.bfloat16), "row").astype(jnp.float32),
        lax.psum(share_second_shift.astype(jnp.bfloat16), "row").astype(jnp.float32),
        lax.psum(share_second_weight.astype(jnp.bfloat16), "row").astype(jnp.float32),
        lax.psum(share_second_bias.astype(jnp.bfloat16), "row").astype(jnp.float32),
        lax.psum(share_mixer_gain.astype(jnp.bfloat16), "row").astype(jnp.float32),
        lax.psum(share_mixer_shift.astype(jnp.bfloat16), "row").astype(jnp.float32),
        lax.psum(share_query_weight.astype(jnp.bfloat16), "row").astype(jnp.float32),
        lax.psum(share_query_bias.astype(jnp.bfloat16), "row").astype(jnp.float32),
        lax.psum(share_key_weight.astype(jnp.bfloat16), "row").astype(jnp.float32),
        lax.psum(share_value_weight.astype(jnp.bfloat16), "row").astype(jnp.float32),
        lax.psum(share_value_bias.astype(jnp.bfloat16), "row").astype(jnp.float32),
        lax.psum(share_output_weight.astype(jnp.bfloat16), "row").astype(jnp.float32),
        lax.psum(share_output_bias.astype(jnp.bfloat16), "row").astype(jnp.float32),
    )
    return (
        decoded,
        latent_grad,
        codebook_grad,
        summed[0],
        summed[1],
        summed[2],
        summed[3],
        summed[4],
        summed[5],
        summed[6],
        summed[7],
        summed[8],
        summed[9],
        summed[10],
        summed[11],
        summed[12],
        summed[13],
        summed[14],
        summed[15],
        summed[16],
        summed[17],
        summed[18],
        summed[19],
        summed[20],
    )


def solution(mesh):
    return jax.shard_map(
        on_device,
        mesh=mesh,
        in_specs=(
            P("dp", "row", None, None),
            P("dp", "row", None),
            P("row", None),
            P(),
            P(),
            P(),
            P(),
            P(),
            P(),
            P(),
            P(),
            P(),
            P(),
            P(),
            P(),
            P(),
            P(),
            P(),
            P(),
            P(),
            P(),
            P(),
            P(),
            P(),
            P("dp", "row", None, None),
        ),
        out_specs=(
            P("dp", "row", None, None),
            P("dp", "row", None, None),
            P(("row", "dp"), None),
            P("dp", None),
            P("dp"),
            P(None, "dp", None),
            P("dp"),
            P("dp"),
            P("dp"),
            P(None, "dp", None),
            P("dp"),
            P("dp"),
            P("dp"),
            P(None, "dp", None),
            P("dp"),
            P("dp"),
            P("dp"),
            P("dp", None),
            P("dp"),
            P("dp", None),
            P("dp", None),
            P("dp"),
            P("dp", None),
            P("dp"),
        ),
        check_vma=False,
    )
```

profile of v0, /device:TPU:0, one launch (start us, length us, event | category | flops | bytes accessed | tf_op | source)
XLA Modules:
  0.0 833.3 jit_solution(18033298385192543896)
XLA Ops:
  8.8 153.2 %all-gather.2.cloned.1.call-done = bf16[16384,256]{1,0:T(8,128)(2,1)} async-done(((bf16[4096,256]{1,0:T(8,128)(2,1)}), bf16[16384,256]{1,0:T(8,128)(2,1)}) %all-gather.2.cloned.1.call-update) | async-done | bytes 8388624 | tf_op jit(solution)/shard_map/all_gather | solution.py:177
  162.0 6.0 fusion.54
  172.1 4.3 collective-permute-done.1
  178.6 10.3 %all-reduce.25 = (f32[8,32]{1,0:T(8,128)S(1)}, f32[8,32]{1,0:T(8,128)S(1)}) all-reduce(f32[8,32]{1,0:T(8,128)S(1)} %reduce_sum.278, f32[8,32]{1,0:T(8,128)S(1)} %reduce_sum.272), channel_id=1, replica_groups=mesh['dp'=8,'row'=4] {'row'}, use_global_device_ids=true, to_apply=%region_5.6 | all-reduce | flops 512 | bytes 4096 | tf_op jit(solution)/shard_map/psum | solution.py:88
  189.7 2.0 collective-permute-start.2
  194.2 4.4 collective-permute-done.3
  199.7 5.6 fusion.34
  206.8 8.6 %all-reduce.24 = (f32[8,32]{1,0:T(8,128)S(1)}, f32[8,32]{1,0:T(8,128)S(1)}) all-reduce(f32[8,32]{1,0:T(8,128)S(1)} %reduce_sum.338, f32[8,32]{1,0:T(8,128)S(1)} %reduce_sum.284), channel_id=1, replica_groups=mesh['dp'=8,'row'=4] {'row'}, use_global_device_ids=true, to_apply=%region_11.12 | all-reduce | flops 512 | bytes 4096 | tf_op jit(solution)/shard_map/psum | solution.py:88
  219.3 4.4 collective-permute-start.4
  225.0 1.8 copy.124
  226.8 4.1 all-to-all-start.2
  236.5 5.6 fusion.24
  243.7 11.1 %all-reduce.23 = (f32[8,32]{1,0:T(8,128)S(1)}, f32[8,32]{1,0:T(8,128)S(1)}) all-reduce(f32[8,32]{1,0:T(8,128)S(1)} %reduce_sum.344, f32[8,32]{1,0:T(8,128)S(1)} %reduce_sum.341), channel_id=1, replica_groups=mesh['dp'=8,'row'=4] {'row'}, use_global_device_ids=true, to_apply=%region_17.18 | all-reduce | flops 512 | bytes 4096 | tf_op jit(solution)/shard_map/psum | solution.py:88
  255.3 2.0 add_convert_fusion.1
  257.4 3.5 all-to-all-start
  260.9 2.6 convert_reduce_fusion.3
  263.5 6.2 all-to-all-done
  282.0 1.7 convert_reduce_fusion.4
  286.0 2.1 multiply_reduce_fusion.9
  290.6 1.9 convert_reduce_fusion.5
  296.5 4.1 all-to-all-start.3
  300.7 2.4 convolution_bitcast_fusion.5
  307.6 4.0 all-to-all-done.3
  311.6 4.1 all-to-all-start.1
  317.8 1.9 bitcast_reduce_fusion
  320.1 12.2 %all-reduce.22 = (f32[8,32]{1,0:T(8,128)S(1)}, f32[8,32]{1,0:T(8,128)S(1)}) all-reduce(f32[8,32]{1,0:T(8,128)S(1)} %reduce_sum.352, f32[8,32]{1,0:T(8,128)S(1)} %reduce_sum.349), channel_id=1, replica_groups=mesh['dp'=8,'row'=4] {'row'}, use_global_device_ids=true, to_apply=%region_26.27 | all-reduce | flops 512 | bytes 4096 | tf_op jit(solution)/shard_map/psum | solution.py:108
  336.1 2.2 convert_reduce_fusion
  339.0 1.9 collective-permute-start.6
  342.2 2.5 convolution_bitcast_fusion.6
  344.8 3.3 collective-permute-done.7
  351.8 4.4 fusion.29
  356.3 2.1 multiply_reduce_fusion
  364.6 9.5 %all-reduce.21 = (f32[8,32]{1,0:T(8,128)}, f32[8,32]{1,0:T(8,128)}) all-reduce(f32[8,32]{1,0:T(8,128)} %reduce_sum.358, f32[8,32]{1,0:T(8,128)} %reduce_sum.355), channel_id=1, replica_groups=mesh['dp'=8,'row'=4] {'row'}, use_global_device_ids=true, to_apply=%region_32.33 | all-reduce | flops 512 | bytes 4096 | tf_op jit(solution)/shard_map/psum | solution.py:108
  376.8 1.6 sub.206
  379.9 1.6 mul.330
  381.5 2.3 convert_reduce_fusion.1
  385.3 4.4 collective-permute-start.8
  393.3 3.7 collective-permute-done.9
  400.8 4.4 fusion.39
  405.2 2.1 multiply_reduce_fusion.1
  413.5 9.2 %all-reduce.20 = (f32[8,32]{1,0:T(8,128)}, f32[8,32]{1,0:T(8,128)}) all-reduce(f32[8,32]{1,0:T(8,128)} %reduce_sum.364, f32[8,32]{1,0:T(8,128)} %reduce_sum.361), channel_id=1, replica_groups=mesh['dp'=8,'row'=4] {'row'}, use_global_device_ids=true, to_apply=%region_38.39 | all-reduce | flops 512 | bytes 4096 | tf_op jit(solution)/shard_map/psum | solution.py:108
  425.4 1.6 sub.212
  428.5 1.6 mul.340
  430.1 4.1 convert_reduce_fusion.2
  434.9 3.6 convolution_bitcast_fusion.2
  438.6 7.3 convolution_bitcast_fusion
  447.0 7.6 convolution_bitcast_fusion.1
  455.6 3.7 collective-permute-start.10
  461.9 4.4 collective-permute-done.11
  475.9 16.3 %reduce-scatter.14.cloned.1.call-done = f32[9,32,512]{2,1,0:T(8,128)} async-done(((f32[9,256,512]{2,1,0:T(8,128)}), f32[9,32,512]{2,1,0:T(8,128)}) %reduce-scatter.14.cloned.1.call-update) | async-done | bytes 589840 | tf_op jit(solution)/shard_map/reduce_scatter | solution.py:390
  492.2 1.8 convert_element_type.321
  494.0 78.6 %reduce-scatter.18.cloned.1.call-done = f32[9,64,512]{2,1,0:T(8,128)} async-done(((f32[9,512,512]{2,1,0:T(8,128)}), f32[9,64,512]{2,1,0:T(8,128)}) %reduce-scatter.18.cloned.1.call-update) | async-done | bytes 1179664 | tf_op jit(solution)/shard_map/reduce_scatter | solution.py:398
  572.6 2.2 convert_element_type.339
  574.8 78.3 %reduce-scatter.16.cloned.1.call-done = f32[9,64,512]{2,1,0:T(8,128)} async-done(((f32[9,512,512]{2,1,0:T(8,128)}), f32[9,64,512]{2,1,0:T(8,128)}) %reduce-scatter.16.cloned.1.call-update) | async-done | bytes 1179664 | tf_op jit(solution)/shard_map/reduce_scatter | solution.py:394
  653.0 2.2 convert_element_type.330
  655.3 13.2 %all_gather.10 = s32[8,12,12]{2,0,1:T(8,128)S(1)} all-gather(s32[8,3,12]{2,0,1:T(8,128)S(1)} %copy-done.45), channel_id=1, replica_groups=mesh['dp'=8,'row'=4] {'row'}, dimensions={1}, use_global_device_ids=true | all-gather | bytes 5760 | tf_op jit(solution)/shard_map/all_gather | solution.py:170
  668.8 16.4 %all_gather.11 = bf16[1152,256]{1,0:T(8,128)(2,1)S(1)} all-gather(bf16[288,256]{1,0:T(8,128)(2,1)S(1)} %reshape.212), channel_id=1, replica_groups=mesh['dp'=8,'row'=4] {'row'}, dimensions={0}, use_global_device_ids=true | all-gather | bytes 737280 | tf_op jit(solution)/shard_map/all_gather | solution.py:358
  685.1 6.9 fusion.1
  698.9 23.7 %all-reduce.19 = (bf16[256]{0:T(256)(128)(2,1)S(1)}, bf16[512]{0:T(512)(128)(2,1)S(1)}, bf16[512]{0:T(512)(128)(2,1)S(1)}, bf16[512]{0:T(512)(128)(2,1)S(1)}, bf...) all-reduce(f32[256]{0:T(256)S(1)} %get-tuple-element.166, ...), channel_id=4, replica_groups=mesh['dp'=8,'row'=4] {'dp'}, use_global_device_ids=true, to_apply=%region_43.44.clone | all-reduce | flops 6400 | bytes 38400
  724.3 18.1 %all-reduce.26 = (bf16[32,256]{1,0:T(8,128)(2,1)S(1)}, bf16[32]{0:T(256)(128)(2,1)S(1)}, bf16[64]{0:T(256)(128)(2,1)S(1)}, bf16[64]{0:T(256)(128)(2,1)S(1)}, bf1...) all-reduce(bf16[32,256]{1,0:T(8,128)(2,1)S(1)} %convert_element_typ, ...), channel_id=1, replica_groups=mesh['dp'=8,'row'=4] {'row'}, use_global_device_ids=true, to_apply=%region_41.42 | all-reduce | flops 8992 | bytes 35968 | tf_op jit(solution)/shard_map/psum | solution.py:412
  749.6 22.2 %all-reduce.30.cloned.1.call-done = (bf16[9,32,512]{2,1,0:T(8,128)(2,1)}, bf16[9,64,512]{2,1,0:T(8,128)(2,1)}, bf16[9,64,512]{2,1,0:T(8,128)(2,1)}, bf16[64,512]...) async-done(((bf16[9,32,512]{2,1,0:T(8,128)(2,1)}, bf16[9,64,512]{2,1,0:T(8,128)(2,1)}, bf16[9,64,512]{2,1,0:T(8,128)(2,1)}, ...) | async-done | bytes 1736720 | tf_op jit(solution)/shard_map/psum | solution.py:414
  777.9 1.8 convert_element_type.322
  779.7 2.3 convert_element_type.331
  783.2 43.1 %reduce-scatter.10.cloned.1.call-done = f32[512,256]{1,0:T(8,128)} async-done(((f32[4096,256]{1,0:T(8,128)}), f32[512,256]{1,0:T(8,128)}) %reduce-scatter.10.cloned.1.call-update) | async-done | bytes 524304 | tf_op jit(solution)/shard_map/reduce_scatter | solution.py:400
  (403 shorter events, 129.2 us)
Async XLA Ops:
  7.2 169.7 %copy-start = (bf16[9,256,512]{2,1,0:T(8,128)(2,1)S(1)}, bf16[9,256,512]{2,1,0:T(8,128)(2,1)}, u32[]{:S(2)}) copy-start(bf16[9,256,512]{2,1,0:T(8,128)(2,1)} %param.30) | copy-start | bytes 7077892
  7.2 154.8 %all-gather.2.cloned.1.call-start = ((), (), s32[]{:S(2)}) async-start(), calls=%async_computation.13 | async-start | bytes 10485760 | tf_op jit(solution)/shard_map/all_gather | solution.py:177
  8.8 159.9 %copy-start.30 = (bf16[256,256]{1,0:T(8,128)(2,1)S(1)}, bf16[256,256]{1,0:T(8,128)(2,1)}, u32[]{:S(2)}) copy-start(bf16[256,256]{1,0:T(8,128)(2,1)} %param.28) | copy-start | bytes 393220
  8.8 159.9 %copy-start.73 = (f32[256]{0:T(256)S(1)}, f32[256]{0:T(256)}, u32[]{:S(2)}) copy-start(f32[256]{0:T(256)} %param.29) | copy-start | bytes 3076
  168.7 8.2 copy-start.74
  168.9 3.2 collective-permute-start
  170.2 6.2 collective-permute-start.1
  176.9 12.4 %copy-start.48 = (f32[512]{0:T(512)S(1)}, f32[512]{0:T(512)}, u32[]{:S(2)}) copy-start(f32[512]{0:T(512)} %param.32) | copy-start | bytes 6148
  177.0 12.4 %copy-start.56 = (f32[512]{0:T(512)S(1)}, f32[512]{0:T(512)}, u32[]{:S(2)}) copy-start(f32[512]{0:T(512)} %param.33) | copy-start | bytes 6148
  189.4 10.0 %copy-start.32 = (f32[8,512]{1,0:T(8,128)}, f32[8,512]{1,0:T(8,128)S(1)}, u32[]{:S(2)}) copy-start(f32[8,512]{1,0:T(8,128)S(1)} %mul.283) | copy-start | bytes 49156
  189.7 4.5 collective-permute-start.2
  191.7 6.9 collective-permute-start.3
  199.7 5.6 copy-start.46
  199.7 6.5 copy-start.42
  219.3 11.7 %collective-permute-start.4 = (bf16[8,1,12,512]{3,2,1,0:T(8,128)(2,1)}, bf16[8,1,12,512]{3,2,1,0:T(8,128)(2,1)}, u32[]{:S(2)}, u32[]{:S(2)}) collective-permute-start(bf16[8,1,12,512]{3,2,1,0:T(8,128)(2,1)} %get-tuple-element.179), channel_id=1, source_target_pairs={{0,1},{1,2},{2,3},{4,5},{5,6},{6,7},{8,9},{9,10},{10,11},{12,13},{... | collective-permute-start | bytes 294920 | tf_op jit(solution)/shard_map/ppermute | solution.py:21
  223.7 8.8 %collective-permute-start.5 = (bf16[8,1,12,512]{3,2,1,0:T(8,128)(2,1)}, bf16[8,1,12,512]{3,2,1,0:T(8,128)(2,1)}, u32[]{:S(2)}, u32[]{:S(2)}) collective-permute-start(bf16[8,1,12,512]{3,2,1,0:T(8,128)(2,1)} %get-tuple-element.180), channel_id=1, source_target_pairs={{1,0},{2,1},{3,2},{5,4},{6,5},{7,6},{9,8},{10,9},{11,10},{13,12},{... | collective-permute-start | bytes 294920 | tf_op jit(solution)/shard_map/ppermute | solution.py:23
  226.8 30.5 %all-to-all-start.2 = ((bf16[8,3,12,512]{3,2,1,0:T(8,128)(2,1)}), bf16[8,3,12,512]{3,2,1,0:T(8,128)(2,1)}, u32[]{:S(2)}, u32[]{:S(2)}) async-start(bf16[8,3,12,512]{3,2,1,0:T(8,128)(2,1)} %copy.124), calls=%async_computation.2 | async-start | bytes 786432 | tf_op jit(solution)/shard_map/all_to_all | solution.py:131
  236.5 5.6 copy-start.47
  236.5 5.6 copy-start.72
  242.1 13.2 %copy-start.50 = (f32[512]{0:T(512)S(1)}, f32[512]{0:T(512)}, u32[]{:S(2)}) copy-start(f32[512]{0:T(512)} %param.40) | copy-start | bytes 6148
  242.2 13.2 %copy-start.70 = (f32[512]{0:T(512)S(1)}, f32[512]{0:T(512)}, u32[]{:S(2)}) copy-start(f32[512]{0:T(512)} %param.41) | copy-start | bytes 6148
  257.4 12.3 %all-to-all-start = ((bf16[8,3,12,512]{3,2,1,0:T(8,128)(2,1)}), bf16[8,3,12,512]{3,2,1,0:T(8,128)(2,1)S(1)}, u32[]{:S(2)}, u32[]{:S(2)}) async-start(bf16[8,3,12,512]{3,2,1,0:T(8,128)(2,1)} %add_convert_fusion.1), calls=%async_computation | async-start | bytes 786432 | tf_op jit(solution)/shard_map/all_to_all | solution.py:131
  260.9 208.9 %reduce-scatter.26.cloned.1.call-start = ((), (), s32[]{:S(2)}) async-start(), calls=%async_computation.22 | async-start | bytes 1179648 | tf_op jit(solution)/shard_map/reduce_scatter | solution.py:408
  270.5 7.9 copy-start.15
  271.8 28.8 %copy-start.9 = (bf16[4,2,3,12,512]{4,1,3,2,0:T(2,128)(2,1)}, bf16[4,2,3,12,512]{4,1,3,2,0:T(2,128)(2,1)S(1)}, u32[]{:S(2)}) copy-start(bf16[4,2,3,12,512]{4,1,3,2,0:T(2,128)(2,1)S(1)} %copy.117) | copy-start | bytes 884740
  279.8 191.5 %reduce-scatter.24.cloned.1.call-start = ((), (), s32[]{:S(2)}) async-start(), calls=%async_computation.21 | async-start | bytes 1179648 | tf_op jit(solution)/shard_map/reduce_scatter | solution.py:406
  288.2 6.5 copy-start.17
  288.2 6.9 copy-start.24
  288.2 6.9 copy-start.31
  294.7 10.4 %copy-start.75 = (f32[512]{0:T(512)S(1)}, f32[512]{0:T(512)}, u32[]{:S(2)}) copy-start(f32[512]{0:T(512)} %param.48) | copy-start | bytes 6148
  295.5 22.3 %copy-start.51 = (f32[512]{0:T(512)S(1)}, f32[512]{0:T(512)}, u32[]{:S(2)}) copy-start(f32[512]{0:T(512)} %param.40) | copy-start | bytes 6148
  296.5 15.1 %all-to-all-start.3 = ((bf16[2,12,12,512]{3,0,2,1:T(2,128)(2,1)}), bf16[2,12,12,512]{3,0,2,1:T(2,128)(2,1)}, u32[]{:S(2)}, u32[]{:S(2)}) async-start(bf16[2,12,12,512]{3,0,2,1:T(2,128)(2,1)} %bitcast.428), calls=%async_computation.3 | async-start | bytes 589824 | tf_op jit(solution)/shard_map/all_to_all | solution.py:135
  300.6 172.2 %reduce-scatter.22.cloned.1.call-start = ((), (), s32[]{:S(2)}) async-start(), calls=%async_computation.20 | async-start | bytes 1179648 | tf_op jit(solution)/shard_map/reduce_scatter | solution.py:405
  311.6 79.3 %all-to-all-start.1 = ((bf16[2,12,12,512]{3,0,2,1:T(2,128)(2,1)}), bf16[2,12,12,512]{3,0,2,1:T(2,128)(2,1)}, u32[]{:S(2)}, u32[]{:S(2)}) async-start(bf16[2,12,12,512]{3,0,2,1:T(2,128)(2,1)} %bitcast.50), calls=%async_computation.1 | async-start | bytes 589824 | tf_op jit(solution)/shard_map/all_to_all | solution.py:135
  315.7 158.7 %reduce-scatter.20.cloned.1.call-start = ((), (), s32[]{:S(2)}) async-start(), calls=%async_computation.19 | async-start | bytes 1179648 | tf_op jit(solution)/shard_map/reduce_scatter | solution.py:403
  339.0 5.8 collective-permute-start.6
  340.9 7.2 collective-permute-start.7
  344.7 147.4 %reduce-scatter.14.cloned.1.call-start = ((), (), s32[]{:S(2)}) async-start(), calls=%async_computation.16 | async-start | bytes 5308416 | tf_op jit(solution)/shard_map/reduce_scatter | solution.py:390
  351.8 4.5 copy-start.3
  385.3 8.0 collective-permute-start.8
  389.7 7.3 collective-permute-start.9
  391.0 7.5 copy-start.5
  430.1 4.9 copy-start.55
  438.6 134.0 %reduce-scatter.18.cloned.1.call-start = ((), (), s32[]{:S(2)}) async-start(), calls=%async_computation.18 | async-start | bytes 10616832 | tf_op jit(solution)/shard_map/reduce_scatter | solution.py:398
  445.9 207.1 %reduce-scatter.16.cloned.1.call-start = ((), (), s32[]{:S(2)}) async-start(), calls=%async_computation.17 | async-start | bytes 10616832 | tf_op jit(solution)/shard_map/reduce_scatter | solution.py:394
  454.6 268.9 %reduce-scatter.12.cloned.1.call-start = ((), (), s32[]{:S(2)}) async-start(), calls=%async_computation.15 | async-start | bytes 294912 | tf_op jit(solution)/shard_map/reduce_scatter | solution.py:388
  455.6 6.2 collective-permute-start.10
  459.4 6.9 collective-permute-start.11
  469.4 185.9 %copy-start.45 = (s32[8,3,12]{2,0,1:T(8,128)S(1)}, s32[8,3,12]{2,0,1:T(8,128)}, u32[]{:S(2)}) copy-start(s32[8,3,12]{2,0,1:T(8,128)} %param.26) | copy-start | bytes 3460
  469.4 302.4 %all-reduce.30.cloned.1.call-start = ((), (), s32[]{:S(2)}) async-start(), calls=%async_computation.23 | async-start | bytes 3473408 | tf_op jit(solution)/shard_map/psum | solution.py:414
  475.9 192.7 %copy-start.28 = (bf16[8,3,12,256]{3,0,2,1:T(8,128)(2,1)S(1)}, bf16[8,3,12,256]{3,0,2,1:T(8,128)(2,1)}, u32[]{:S(2)}) copy-start(bf16[8,3,12,256]{3,0,2,1:T(8,128)(2,1)} %param.25) | copy-start | bytes 442372
  655.2 171.1 %reduce-scatter.10.cloned.1.call-start = ((), (), s32[]{:S(2)}) async-start(), calls=%async_computation.14 | async-start | bytes 4718592 | tf_op jit(solution)/shard_map/reduce_scatter | solution.py:400
  692.0 6.7 copy-start.60
  692.0 6.7 copy-start.61
  692.1 6.7 copy-start.62
  692.1 6.7 copy-start.63
  692.1 6.7 copy-start.64
  692.1 6.7 copy-start.65
  692.1 6.7 copy-start.66
  692.1 6.7 copy-start.67
  692.1 6.7 copy-start.68
  692.1 6.7 copy-start.69
  692.1 6.7 copy-start.71
  771.8 10.2 %copy-start.29 = (bf16[9,64,512]{2,1,0:T(8,128)(2,1)S(1)}, bf16[9,64,512]{2,1,0:T(8,128)(2,1)}, u32[]{:S(2)}) copy-start(bf16[9,64,512]{2,1,0:T(8,128)(2,1)} %get-tuple-element.153) | copy-start | bytes 1769476
  (40 other events, 99.5 us)
Sparse Core Ops, SparseCore 0:
  9.6 152.3 all-gather.1
  279.9 35.0 reduce-scatter.25
  318.2 35.9 reduce-scatter.23
  357.9 36.0 reduce-scatter.21
  397.5 36.0 reduce-scatter.19
  438.7 53.4 reduce-scatter.13
  496.1 76.4 reduce-scatter.17
  576.5 76.4 reduce-scatter.15
  656.3 33.5 reduce-scatter.11
  694.5 77.2 all-reduce.29
  776.1 50.1 reduce-scatter.9
where the time goes:
time: 845 us; the launch traced here: 833 us
  waiting for transfers between devices  427 us (51%)
  blocking collectives  132 us (16%)
  other arithmetic  81.8 us (10%)
  matrix products  80.9 us (10%)
  local copies, waits for them, and re-layouts  51.5 us (6%)
  starting transfers between devices  42 us (5%)
  between operations  17.7 us (2%)
    all_gather x1, waiting for transfers between devices, on_device(): whole_book = lax.all_gather(codebook, 'row', axis=0, tiled=True)  153 us
    reduce_scatter x1, waiting for transfers between devices, on_device(): lax.psum_scatter(grad_second_weight, 'dp', scatter_dimension=1, tiled=True)  78.6 us
    reduce_scatter x1, waiting for transfers between devices, on_device(): lax.psum_scatter(grad_first_weight, 'dp', scatter_dimension=1, tiled=True)  78.3 us
    reduce_scatter x1, waiting for transfers between devices, on_device(): lax.psum_scatter(grad_book, 'dp', scatter_dimension=0, tiled=True)  43.1 us
    psum x3, blocking collectives, norm_back(): first_sum, second_sum = lax.psum((first_sum, second_sum), 'row')  30.9 us
    psum x3, blocking collectives, group_stats(): first_sum, second_sum = lax.psum((first_sum, second_sum), 'row')  30 us
    unnamed x1, blocking collectives  23.7 us
    psum x1, waiting for transfers between devices, on_device(): lax.psum(share_entry_weight.astype(jnp.bfloat16), 'row').astype(jnp.float32)  22.2 us
  transfers between devices with their start and end apart: 27, of which 17 were waited for; matrix products, arithmetic and copies ran while one was open for 21% of the time, Pallas kernels for 0%

commit v1 on v0

v1 whole, which is shorter than its diff:
```python
import jax
import jax.numpy as jnp
from jax import lax
from jax.sharding import PartitionSpec as P

GROUPS = 32
EPSILON = 1e-06
BETA_COMMIT = 0.25
F32 = jnp.float32
BF16 = jnp.bfloat16


def bfloat(tensor):
    return tensor.astype(BF16)


def rounded(tensor):
    return lax.reduce_precision(tensor, 8, 7).astype(BF16)


def to_images(tensor):
    return lax.all_to_all(tensor, "row", split_axis=0, concat_axis=1, tiled=True)


def to_rows(tensor):
    return lax.all_to_all(tensor, "row", split_axis=1, concat_axis=0, tiled=True)


def gather_rows(tensor):
    count = lax.axis_size("row")
    copies = jnp.broadcast_to(tensor[None], (count,) + tensor.shape)
    got = lax.all_to_all(copies, "row", split_axis=0, concat_axis=0, tiled=True)
    got = jnp.moveaxis(got, 0, 1)
    return got.reshape((tensor.shape[0], count * tensor.shape[1]) + tensor.shape[2:])


def reduce_dp(blocks):
    count, rows, lanes = blocks.shape
    core = lax.rem(lax.axis_index("dp"), 2)
    pairs = bfloat(blocks).reshape(count // 2, 2, rows, lanes)
    mine = lax.dynamic_index_in_dim(pairs, core, 1, keepdims=False)
    other = lax.dynamic_index_in_dim(pairs, 1 - core, 1, keepdims=False)
    got = lax.ppermute(other, "dp", [(i, i ^ 1) for i in range(count)])
    both = bfloat(mine.astype(F32) + got.astype(F32))
    groups = [[2 * i + c for i in range(count // 2)] for c in range(2)]
    parts = lax.all_to_all(both, "dp", 0, 0, axis_index_groups=groups, tiled=True)
    return jnp.sum(parts.astype(F32), axis=0)


def reduce_row(part):
    count = lax.axis_size("row")
    me = lax.axis_index("row")
    half = count // 2
    for k in range(half - 1):
        got = lax.ppermute(rounded(part), "row", [(k, k + 1), (count - 1 - k, count - 2 - k)])
        part = part + got.astype(F32)
    low = rounded(part)
    got = lax.ppermute(low, "row", [(half - 1, half), (half, half - 1)])
    total = rounded(low.astype(F32) + got.astype(F32))
    for k in range(half - 1, 0, -1):
        got = lax.ppermute(total, "row", [(k, k - 1), (count - 1 - k, count - k)])
        total = jnp.where((me == k - 1) | (me == count - k), got, total)
    return total.astype(F32)


def patches(tensor, reverse):
    height, width = tensor.shape[1], tensor.shape[2]
    padded = jnp.pad(tensor, ((0, 0), (1, 1), (1, 1), (0, 0)))
    tap_list = []
    for row_tap in range(3):
        for col_tap in range(3):
            y = 2 - row_tap if reverse else row_tap
            x = 2 - col_tap if reverse else col_tap
            tap_list.append(padded[:, y : y + height, x : x + width, :])
    return jnp.stack(tap_list, axis=3)


def conv_apply(columns, kernel):
    return jnp.einsum("bhwtc,tcf->bhwf", columns, kernel, preferred_element_type=F32)


def conv_back(columns, kernel):
    return jnp.einsum("bhwtf,tcf->bhwc", columns, kernel, preferred_element_type=F32)


def kernel_grad(columns, gradient):
    return jnp.einsum("bhwtc,bhwf->tcf", columns, gradient, preferred_element_type=F32)


def group_view(tensor):
    batch_size, height, width, channel_count = tensor.shape
    return tensor.reshape(batch_size, height * width, GROUPS, channel_count // GROUPS)


def group_stats(tensor):
    grouped = group_view(tensor)
    average = jnp.mean(grouped, axis=(1, 3))
    variance = jnp.mean(jnp.square(grouped - average[:, None, :, None]), axis=(1, 3))
    return (average, lax.rsqrt(variance + EPSILON))


def normalize(tensor, average, inverse):
    grouped = group_view(tensor)
    scaled = (grouped - average[:, None, :, None]) * inverse[:, None, :, None]
    return scaled.reshape(tensor.shape)


def norm_back(gradient, standard, inverse, gain_vec):
    gain_grad = jnp.sum(gradient * standard, axis=(0, 1, 2))
    shift_grad = jnp.sum(gradient, axis=(0, 1, 2))
    scaled = group_view(gradient * gain_vec)
    normal = group_view(standard)
    first = jnp.mean(scaled, axis=(1, 3))
    second = jnp.mean(scaled * normal, axis=(1, 3))
    out = (scaled - first[:, None, :, None] - normal * second[:, None, :, None]) * inverse[
        :, None, :, None
    ]
    return (out.reshape(gradient.shape), gain_grad, shift_grad)


def silu_slope(pre_act):
    logistic = jax.nn.sigmoid(pre_act)
    return logistic * (1.0 + pre_act * (1.0 - logistic))


def mm(pattern, a, b):
    return jnp.einsum(pattern, a, b, preferred_element_type=F32)


def on_device(
    latent,
    codes,
    codebook,
    post_weight,
    post_bias,
    entry_weight,
    entry_bias,
    first_gain,
    first_shift,
    first_weight,
    first_bias,
    second_gain,
    second_shift,
    second_weight,
    second_bias,
    mixer_gain,
    mixer_shift,
    query_weight,
    query_bias,
    key_weight,
    value_weight,
    value_bias,
    projection_output_weight,
    projection_output_bias,
    cotangent,
):
    batch, rows_local, width, embed = latent.shape
    channels = entry_weight.shape[2]
    row_count = lax.axis_size("row")
    dp_count = lax.axis_size("dp")
    owned = codebook.shape[0]
    height = rows_local * row_count
    crops = batch // row_count
    sequence = height * width
    tokens_all = batch * sequence
    me = lax.axis_index("row")

    all_codes = lax.all_gather(codes, "row", axis=1, tiled=True).reshape(tokens_all)
    one_hot = (
        all_codes[:, None] - me * owned == lax.broadcasted_iota(jnp.int32, (tokens_all, owned), 1)
    ).astype(BF16)
    found = bfloat(jnp.dot(one_hot, codebook, preferred_element_type=F32))
    pieces = lax.all_to_all(
        found.reshape(row_count, crops * sequence, embed), "row", 0, 0, tiled=True
    )
    quant = bfloat(jnp.sum(pieces.astype(F32), axis=0))
    cot = to_images(cotangent)
    latent_all = gather_rows(latent).reshape(tokens_all, embed)
    difference = bfloat(2.0 * (found.astype(F32) - latent_all.astype(F32)))
    grad_book = jnp.einsum("pk,pe->ke", one_hot, difference, preferred_element_type=F32)
    codebook_grad = lax.psum_scatter(bfloat(grad_book), "dp", scatter_dimension=0, tiled=True).astype(F32)
    latent_mine = lax.dynamic_slice_in_dim(latent_all, me * crops * sequence, crops * sequence, 0)

    post = bfloat(jnp.dot(quant, post_weight, preferred_element_type=F32) + post_bias).reshape(
        crops, height, width, embed
    )
    post_cols = patches(post, False)
    stream = conv_apply(post_cols, entry_weight) + entry_bias
    average_one, inverse_one = group_stats(stream)
    standard_one = normalize(stream, average_one, inverse_one)
    pre_one = standard_one * first_gain + first_shift
    cols_one = patches(bfloat(jax.nn.silu(pre_one)), False)
    middle = conv_apply(cols_one, first_weight) + first_bias
    average_two, inverse_two = group_stats(middle)
    standard_two = normalize(middle, average_two, inverse_two)
    pre_two = standard_two * second_gain + second_shift
    cols_two = patches(bfloat(jax.nn.silu(pre_two)), False)
    hidden = stream + (conv_apply(cols_two, second_weight) + second_bias)
    average_mix, inverse_mix = group_stats(hidden)
    standard_mix = normalize(hidden, average_mix, inverse_mix)
    tokens = bfloat(standard_mix * mixer_gain + mixer_shift).reshape(crops, sequence, channels)
    cot_seq = cot.reshape(crops, sequence, channels)
    query = bfloat(mm("bsc,cd->bsd", tokens, query_weight) + query_bias)
    key = bfloat(mm("bsc,cd->bsd", tokens, key_weight))
    value = bfloat(mm("bsc,cd->bsd", tokens, value_weight) + value_bias)
    scale = channels ** (-0.5)
    logits = mm("nsw,nlw->nsl", query, key) * scale
    peak = jnp.max(logits, axis=2, keepdims=True)
    exponents = jnp.exp(logits - peak)
    probs = exponents / jnp.sum(exponents, axis=2, keepdims=True)
    weights = bfloat(probs)
    attended = bfloat(mm("nsl,nlw->nsw", weights, value))
    result = bfloat(mm("nsw,wt->nst", attended, projection_output_weight) + projection_output_bias)
    decoded = to_rows(bfloat(hidden + result.astype(F32).reshape(hidden.shape)))

    grad_output_weight = mm("nst,nsx->tx", attended, cot_seq)
    grad_output_bias = jnp.sum(cot_seq.astype(F32), axis=(0, 1))
    grad_attended = bfloat(mm("nsu,iu->nsi", cot_seq, projection_output_weight))
    grad_weights = mm("nsw,nlw->nsl", grad_attended, value)
    grad_value = bfloat(mm("nsl,nsw->nlw", weights, grad_attended))
    grad_scores = bfloat(
        probs * (grad_weights - jnp.sum(grad_weights * probs, axis=2, keepdims=True))
    )
    grad_query = bfloat(mm("nsl,nlw->nsw", grad_scores, key) * scale)
    grad_key = bfloat(mm("nsl,nsw->nlw", grad_scores, query) * scale)
    grad_query_weight = mm("bsc,bsd->cd", tokens, grad_query)
    grad_query_bias = jnp.sum(grad_query.astype(F32), axis=(0, 1))
    grad_key_weight = mm("bsc,bsd->cd", tokens, grad_key)
    grad_value_weight = mm("bsc,bsd->cd", tokens, grad_value)
    grad_value_bias = jnp.sum(grad_value.astype(F32), axis=(0, 1))
    grad_tokens = (
        mm("bsd,cd->bsc", grad_query, query_weight)
        + mm("bsd,cd->bsc", grad_key, key_weight)
        + mm("bsd,cd->bsc", grad_value, value_weight)
    )
    grad_normed = bfloat(grad_tokens).reshape(hidden.shape).astype(F32)
    grad_mix, grad_mixer_gain, grad_mixer_shift = norm_back(
        grad_normed, standard_mix, inverse_mix, mixer_gain
    )
    grad_hidden = cot.astype(F32) + grad_mix
    grad_branch = bfloat(grad_hidden)
    grad_second_weight = kernel_grad(cols_two, grad_branch)
    grad_second_bias = jnp.sum(grad_branch.astype(F32), axis=(0, 1, 2))
    grad_act_two = conv_back(patches(grad_branch, True), second_weight)
    grad_middle_full, grad_second_gain, grad_second_shift = norm_back(
        grad_act_two * silu_slope(pre_two), standard_two, inverse_two, second_gain
    )
    grad_middle = bfloat(grad_middle_full)
    grad_first_weight = kernel_grad(cols_one, grad_middle)
    grad_first_bias = jnp.sum(grad_middle.astype(F32), axis=(0, 1, 2))
    grad_act_one = conv_back(patches(grad_middle, True), first_weight)
    grad_stream_norm, grad_first_gain, grad_first_shift = norm_back(
        grad_act_one * silu_slope(pre_one), standard_one, inverse_one, first_gain
    )
    grad_stream = bfloat(grad_hidden + grad_stream_norm)
    grad_entry_weight = kernel_grad(post_cols, grad_stream)
    grad_entry_bias = jnp.sum(grad_stream.astype(F32), axis=(0, 1, 2))
    grad_post = bfloat(conv_back(patches(grad_stream, True), entry_weight)).reshape(
        crops * sequence, embed
    )
    grad_post_weight = mm("pe,pf->ef", quant, grad_post)
    grad_post_bias = jnp.sum(grad_post.astype(F32), axis=0)
    grad_latent = mm("pf,ef->pe", grad_post, post_weight) + 2.0 * BETA_COMMIT * (
        latent_mine.astype(F32) - quant.astype(F32)
    )
    latent_grad = to_rows(bfloat(grad_latent).reshape(crops, height, width, embed)).astype(F32)

    def taps(grad):
        count, inner, outer = grad.shape
        return (
            grad.reshape(count, dp_count, inner // dp_count, outer)
            .transpose(1, 0, 2, 3)
            .reshape(dp_count, count * inner // dp_count, outer)
        )

    def whole(grad):
        return grad.reshape(dp_count, -1, channels)

    vectors = jnp.concatenate(
        [
            v.reshape(dp_count, -1)
            for v in (
                grad_entry_bias,
                grad_first_gain,
                grad_first_shift,
                grad_first_bias,
                grad_second_gain,
                grad_second_shift,
                grad_second_bias,
                grad_mixer_gain,
                grad_mixer_shift,
                grad_query_bias,
                grad_value_bias,
                grad_output_bias,
                grad_post_bias,
            )
        ],
        axis=1,
    )
    size = vectors.shape[1]
    lines = -(-size // channels)
    vectors = jnp.pad(vectors, ((0, 0), (0, lines * channels - size))).reshape(
        dp_count, lines, channels
    )

    parts_a = [whole(g) for g in (grad_output_weight, grad_query_weight, grad_key_weight, grad_value_weight)]
    parts_a.append(taps(grad_second_weight))
    sum_a = reduce_row(reduce_dp(jnp.concatenate(parts_a, axis=1)))
    sum_b = reduce_row(reduce_dp(taps(grad_first_weight)))
    parts_c = [taps(grad_entry_weight), whole(grad_post_weight), vectors]
    sum_c = reduce_row(reduce_dp(jnp.concatenate(parts_c, axis=1)))

    share = channels // dp_count
    o_w, q_w, k_w, v_w = (sum_a[i * share : (i + 1) * share] for i in range(4))
    second_w = sum_a[4 * share :].reshape(9, share, channels)
    first_w = sum_b.reshape(9, share, channels)
    e_share = embed // dp_count
    entry_w = sum_c[: 9 * e_share].reshape(9, e_share, channels)
    post_rows = e_share * embed // channels
    post_w = sum_c[9 * e_share : 9 * e_share + post_rows].reshape(e_share, embed)
    flat = sum_c[9 * e_share + post_rows :].reshape(-1)
    vec = [flat[i * share : (i + 1) * share] for i in range(12)]
    post_b = flat[12 * share : 12 * share + e_share]
    return (
        decoded,
        latent_grad,
        codebook_grad,
        post_w,
        post_b,
        entry_w,
        vec[0],
        vec[1],
        vec[2],
        first_w,
        vec[3],
        vec[4],
        vec[5],
        second_w,
        vec[6],
        vec[7],
        vec[8],
        q_w,
        vec[9],
        k_w,
        v_w,
        vec[10],
        o_w,
        vec[11],
    )


def solution(mesh):
    def cells(depth):
        return P("dp", "row", *([None] * depth))

    return jax.shard_map(
        on_device,
        mesh=mesh,
        in_specs=(cells(2), cells(1), P("row", None)) + (P(),) * 21 + (cells(2),),
        out_specs=(
            cells(2),
            cells(2),
            P(("row", "dp"), None),
            P("dp", None),
            P("dp"),
            P(None, "dp", None),
            P("dp"),
            P("dp"),
            P("dp"),
            P(None, "dp", None),
            P("dp"),
            P("dp"),
            P("dp"),
            P(None, "dp", None),
            P("dp"),
            P("dp"),
            P("dp"),
            P("dp", None),
            P("dp"),
            P("dp", None),
            P("dp", None),
            P("dp"),
            P("dp", None),
            P("dp"),
        ),
        check_vma=False,
    )
```

time: 845 us -> 429 us (0.51)
  waiting for transfers between devices: 427 us -> 77.3 us
  blocking collectives: 132 us -> 17.8 us
  local copies, waits for them, and re-layouts: 51.5 us -> 100 us
  other arithmetic: 81.8 us -> 62.2 us
  starting transfers between devices: 42 us -> 59.3 us
    reduce_scatter x9 -> x1, waiting for transfers between devices: 216 us -> 0.02 us  [on_device(): lax.psum_scatter(bfloat(grad_book), 'dp', scatter_dimension=0, tiled=True)]
    all_gather x1 -> x0, waiting for transfers between devices: 153 us -> none  [on_device(): whole_book = lax.all_gather(codebook, 'row', axis=0, tiled=True)]
    psum x7 -> x0, blocking collectives: 79.1 us -> none  [the longest x3 30.9 us: norm_back(): first_sum, second_sum = lax.psum((first_sum, second_sum), 'row')]
    dot_general x0 -> x6, local copies, waits for them, and re-layouts: none -> 29.4 us  [the longest x3 23.9 us: kernel_grad(): jnp.einsum('bhwtc,bhwf->tcf', columns, gradient, preferred_element_type=F32)]
    all_to_all x0 -> x5, waiting for transfers between devices: none -> 24 us  [the longest x3 15.6 us: reduce_dp(): lax.all_to_all(both, 'dp', 0, 0, axis_index_groups=groups, tiled=True)]
    unnamed x1 -> x0, blocking collectives: 23.7 us -> none
    all_to_all x2, waiting for transfers between devices: 3.99 us -> 26.8 us  [to_rows(): lax.all_to_all(tensor, 'row', split_axis=1, concat_axis=0, tiled=True)]
    all_to_all x0 -> x5, starting transfers between devices: none -> 22.5 us  [the longest x3 13.7 us: reduce_dp(): lax.all_to_all(both, 'dp', 0, 0, axis_index_groups=groups, tiled=True)]
  transfers between devices with their start and end apart: 27 -> 21, of which waited for: 17 -> 8; matrix products, arithmetic and copies ran while one was open for 21% -> 56% of each run, Pallas kernels for 0% -> 0%
where the time goes in v1:
time: 429 us; the launch traced here: 421 us
  local copies, waits for them, and re-layouts  100 us (23%)
  matrix products  88.3 us (21%)
  waiting for transfers between devices  77.3 us (18%)
  other arithmetic  62.2 us (14%)
  starting transfers between devices  59.3 us (14%)
  blocking collectives  17.8 us (4%)
  between operations  15.9 us (4%)
    dot_general x20, matrix products, mm(): return jnp.einsum(pattern, a, b, preferred_element_type=F32)  30.2 us
    all_to_all x2, waiting for transfers between devices, to_rows(): lax.all_to_all(tensor, 'row', split_axis=1, concat_axis=0, tiled=True)  26.8 us
    ppermute x3, waiting for transfers between devices, reduce_row(): got = lax.ppermute(total, 'row', [(k, k - 1), (count - 1 - k, count - k)])  26.1 us
    dot_general x3, local copies, waits for them, and re-layouts, kernel_grad(): jnp.einsum('bhwtc,bhwf->tcf', columns, gradient, preferred_element_type=F32)  23.9 us
    dot_general x3, matrix products, kernel_grad(): jnp.einsum('bhwtc,bhwf->tcf', columns, gradient, preferred_element_type=F32)  20 us
    all_gather x1, blocking collectives, on_device(): lax.all_gather(codes, 'row', axis=1, tiled=True).reshape(tokens_all)  17.8 us
    unnamed x185, local copies, waits for them, and re-layouts  15.7 us
    all_to_all x3, waiting for transfers between devices, reduce_dp(): lax.all_to_all(both, 'dp', 0, 0, axis_index_groups=groups, tiled=True)  15.6 us
  transfers between devices with their start and end apart: 21, of which 8 were waited for; matrix products, arithmetic and copies ran while one was open for 56% of the time, Pallas kernels for 0%

profile of v1, /device:TPU:0, one launch (start us, length us, event | category | flops | bytes accessed | tf_op | source)
XLA Modules:
  0.0 421.3 jit_solution(4559944243845215974)
XLA Ops:
  7.2 2.0 copy.300
  9.2 6.3 %all-to-all-start.2 = ((bf16[8,3,12,512]{3,2,1,0:T(8,128)(2,1)}), bf16[8,3,12,512]{3,2,1,0:T(8,128)(2,1)S(1)}, u32[]{:S(2)}, u32[]{:S(2)}) async-start(bf16[8,3,12,512]{3,2,1,0:T(8,128)(2,1)} %copy.300), calls=%async_computation.2 | async-start | bytes 786432 | tf_op jit(solution)/shard_map/all_to_all | solution.py:22
  15.5 17.8 %all_gather.3 = s32[8,12,12]{2,0,1:T(8,128)S(1)} all-gather(s32[8,3,12]{2,0,1:T(8,128)} %param.26), channel_id=1, replica_groups=mesh['dp'=8,'row'=4] {'row'}, dimensions={1}, use_global_device_ids=true | all-gather | bytes 5760 | tf_op jit(solution)/shard_map/all_gather | solution.py:168
  33.4 5.7 %fusion.34 = bf16[1152,256]{1,0:T(8,128)(2,1)} fusion(bf16[4096,256]{1,0:T(8,128)(2,1)} %param.27, s32[1152]{0:T(1024)S(1)} %sub.164), kind=kOutput, calls=%fused_computation.39 | convolution fusion | flops 2420932608 | bytes 2691584 | tf_op jit(solution)/shard_map/dot_general | solution.py:172
  39.2 4.3 %all-to-all-start = ((bf16[4,288,256]{2,1,0:T(8,128)(2,1)}), bf16[4,288,256]{2,1,0:T(8,128)(2,1)}, u32[]{:S(2)}, u32[]{:S(2)}) async-start(bf16[4,288,256]{2,1,0:T(8,128)(2,1)} %bitcast), calls=%async_computation | async-start | bytes 1179648 | tf_op jit(solution)/shard_map/all_to_all | solution.py:173
  45.9 2.1 convolution_convert_fusion.1
  48.0 8.5 %all-to-all-done = bf16[4,288,256]{2,1,0:T(8,128)(2,1)} async-done(((bf16[4,288,256]{2,1,0:T(8,128)(2,1)}), bf16[4,288,256]{2,1,0:T(8,128)(2,1)}, u32[]{:S(2)}, u32[]{:S(2)}) %all-to-all-start) | async-done | bytes 589856 | tf_op jit(solution)/shard_map/all_to_all | solution.py:173
  57.4 4.5 %all-to-all-start.3 = ((bf16[4,8,3,12,256]{4,1,3,2,0:T(8,128)(2,1)}), bf16[4,8,3,12,256]{4,1,3,2,0:T(8,128)(2,1)}, u32[]{:S(2)}, u32[]{:S(2)}) async-start(bf16[4,8,3,12,256]{4,1,3,2,0:T(8,128)(2,1)} %broadcast_in_dim.2), calls=%async_computation.3 | async-start | bytes 1179648 | tf_op jit(solution)/shard_map/all_to_all | solution.py:32
  68.0 5.6 %fusion.18 = f32[2,12,12,512,1]{3,2,0,1,4:T(8,128)S(1)} fusion(bf16[9,512,512]{2,1,0:T(8,128)(2,1)} %param.34, bf16[2,12,12,9,512]{4,2,1,0,3:T(8,128)(2,1)S(1)} %bitcast_dynamic-update-slice_fusion.36), kind=kOutput, calls=%fused_computation.25 | convolution fusion | flops 1358954496 | bytes 7962624 | tf_op jit(solution)/shard_map/bhwtc,tcf->bhwf/dot_general | solution.py:79
  76.1 5.6 %fusion.22 = f32[2,12,12,512,1]{3,2,0,1,4:T(8,128)S(1)} fusion(bf16[9,512,512]{2,1,0:T(8,128)(2,1)} %param.38, bf16[2,12,12,9,512]{4,2,1,0,3:T(8,128)(2,1)S(1)} %bitcast_dynamic-update-slice_fusion.27), kind=kOutput, calls=%fused_computation.29 | convolution fusion | flops 1358954496 | bytes 7962624 | tf_op jit(solution)/shard_map/bhwtc,tcf->bhwf/dot_general | solution.py:79
  92.8 2.5 fusion.116
  95.3 2.0 convolution_convert_fusion.2
  104.6 2.2 fusion.105
  107.8 4.4 %fusion.20 = f32[2,12,12,512,1]{3,2,0,1,4:T(8,128)S(1)} fusion(bf16[9,512,512]{2,1,0:T(8,128)(2,1)} %param.38, bf16[2,12,12,9,512]{4,2,1,0,3:T(8,128)(2,1)S(1)} %bitcast_dynamic-update-slice_fusion.18), kind=kOutput, calls=%fused_computation.27 | convolution fusion | flops 1358954496 | bytes 7962624 | tf_op jit(solution)/shard_map/bhwtf,tcf->bhwc/dot_general | solution.py:83
  112.2 2.1 multiply_reduce_fusion
  115.0 2.2 fusion.107
  118.2 4.4 %fusion.16 = f32[2,12,12,512,1]{3,2,0,1,4:T(8,128)S(1)} fusion(bf16[9,512,512]{2,1,0:T(8,128)(2,1)} %param.34, bf16[2,12,12,9,512]{4,2,1,0,3:T(8,128)(2,1)S(1)} %bitcast_dynamic-update-slice_fusion.9), kind=kOutput, calls=%fused_computation.23 | convolution fusion | flops 1358954496 | bytes 7962624 | tf_op jit(solution)/shard_map/bhwtf,tcf->bhwc/dot_general | solution.py:83
  122.6 2.0 multiply_reduce_fusion.1
  126.2 8.4 %reshape.411 = bf16[9,8,64,2,12,12]{2,1,5,4,3,0:T(8,128)(2,1)} reshape(bf16[9,512,2,12,12]{1,4,3,2,0:T(8,128)(2,1)} %bitcast.399) | data formatting | bytes 5308416 | tf_op jit(solution)/shard_map/bhwtc,bhwf->tcf/dot_general | solution.py:87
  134.5 6.8 %fusion.13 = bf16[8,9,64,512]{3,2,0,1:T(8,128)(2,1)S(1)} fusion(bf16[9,8,64,2,12,12]{2,1,5,4,3,0:T(8,128)(2,1)} %reshape.411, bf16[2,12,12,512]{3,2,1,0:T(8,128)(2,1)S(1)} %get-tuple-element.39), kind=kOutput, calls=%fused_computation.18 | convolution fusion | flops 1361313792 | bytes 7667712 | tf_op jit(solution)/shard_map/bhwtc,bhwf->tcf/dot_general | solution.py:87
  142.0 2.1 copy-done.8
  145.6 2.1 dot_general.145
  149.0 2.2 copy.327
  151.1 2.4 fusion.46
  153.6 2.4 fusion.48
  156.0 2.3 fusion.50
  159.6 8.3 %reshape.412 = bf16[9,8,64,2,12,12]{2,1,5,4,3,0:T(8,128)(2,1)} reshape(bf16[9,512,2,12,12]{1,4,3,2,0:T(8,128)(2,1)} %bitcast.400) | data formatting | bytes 5308416 | tf_op jit(solution)/shard_map/bhwtc,bhwf->tcf/dot_general | solution.py:87
  167.9 6.7 %fusion.14 = bf16[8,9,64,512]{3,2,0,1:T(8,128)(2,1)S(1)} fusion(bf16[9,8,64,2,12,12]{2,1,5,4,3,0:T(8,128)(2,1)} %reshape.412, bf16[2,12,12,512]{3,2,1,0:T(8,128)(2,1)S(1)} %get-tuple-element.37), kind=kOutput, calls=%fused_computation.19 | convolution fusion | flops 1361313792 | bytes 7667712 | tf_op jit(solution)/shard_map/bhwtc,bhwf->tcf/dot_general | solution.py:87
  175.1 2.5 constant_dynamic-update-slice_fusion
  177.6 4.0 dynamic-slice_bitcast_fusion
  183.7 2.9 fusion.108
  189.8 4.5 %fusion.15 = bf16[4,576,512]{2,1,0:T(8,128)(2,1)} fusion(bf16[4,576,512]{2,1,0:T(8,128)(2,1)} %collective-permute-done.4, bf16[4,2,576,512]{3,2,1,0:T(8,128)(2,1)} %bitcast.391, s32[]{:T(128)S(6)} %select_n.42), kind=kLoop, calls=%fused_computation.21 | loop fusion | flops 4718592 | bytes 7077892 | tf_op jit(solution)/shard_map/convert_element_type | solution.py:14
  194.3 4.7 %all-to-all-start.6 = ((bf16[4,576,512]{2,1,0:T(8,128)(2,1)}), bf16[4,576,512]{2,1,0:T(8,128)(2,1)}, u32[]{:S(2)}, u32[]{:S(2)}) async-start(bf16[4,576,512]{2,1,0:T(8,128)(2,1)} %fusion.15), calls=%async_computation.7 | async-start | bytes 4718592 | tf_op jit(solution)/shard_map/all_to_all | solution.py:46
  201.4 2.3 copy.296
  204.6 3.1 fusion.24
  219.3 2.8 fusion.71
  227.9 7.2 %reshape.410 = bf16[9,8,32,2,12,12]{2,1,5,0,4,3:T(8,128)(2,1)} reshape(bf16[9,256,2,12,12]{1,4,0,3,2:T(8,128)(2,1)} %bitcast.413) | data formatting | bytes 2654208 | tf_op jit(solution)/shard_map/bhwtc,bhwf->tcf/dot_general | solution.py:87
  235.1 5.8 %fusion.11 = bf16[4,832,512]{2,1,0:T(8,128)(2,1)} fusion(bf16[4,832,512]{2,1,0:T(8,128)(2,1)} %collective-permute-done.8, bf16[4,2,832,512]{3,2,1,0:T(8,128)(2,1)} %constant_dynamic-update-slice_fusion, s32[]{:T(128)S(6)} %select_n.42), kind=kLoop, calls=%fused_computation.15 | loop fusion | flops 6815744 | bytes 10223620 | tf_op jit(solution)/shard_map/convert_element_type | solution.py:14
  240.9 4.7 %all-to-all-start.7 = ((bf16[4,832,512]{2,1,0:T(8,128)(2,1)}), bf16[4,832,512]{2,1,0:T(8,128)(2,1)}, u32[]{:S(2)}, u32[]{:S(2)}) async-start(bf16[4,832,512]{2,1,0:T(8,128)(2,1)} %fusion.11), calls=%async_computation.8 | async-start | bytes 6815744 | tf_op jit(solution)/shard_map/all_to_all | solution.py:46
  245.6 6.5 %fusion.36 = bf16[8,9,32,512]{3,2,0,1:T(8,128)(2,1)S(1)} fusion(bf16[9,8,32,2,12,12]{2,1,5,0,4,3:T(8,128)(2,1)} %reshape.410, bf16[2,12,12,512]{3,2,1,0:T(8,128)(2,1)S(1)} %get-tuple-element.41), kind=kOutput, calls=%fused_computation.44 | convolution fusion | flops 680656896 | bytes 3981312 | tf_op jit(solution)/shard_map/bhwtc,bhwf->tcf/dot_general | solution.py:87
  254.3 1.8 copy.319
  258.3 7.9 %fusion.12 = bf16[4096,256]{1,0:T(8,128)(2,1)} fusion(s32[1152]{0:T(1024)S(1)} %copy-done.56, bf16[1152,256]{1,0:T(8,128)(2,1)} %reshape_reshape.3, bf16[1152,256]{1,0:T(8,128)(2,1)} %fusion.34), kind=kOutput, calls=%fused_computation.17 | convolution fusion | flops 2423160832 | bytes 3281408 | tf_op jit(solution)/shard_map/pk,pe->ke/dot_general | solution.py:180
  266.2 3.1 fusion.35
  269.3 2.1 convert_reduce_fusion.1
  271.5 13.5 %all-to-all-done.7 = bf16[4,832,512]{2,1,0:T(8,128)(2,1)} async-done(((bf16[4,832,512]{2,1,0:T(8,128)(2,1)}), bf16[4,832,512]{2,1,0:T(8,128)(2,1)}, u32[]{:S(2)}, u32[]{:S(2)}) %all-to-all-start.7) | async-done | bytes 3407904 | tf_op jit(solution)/shard_map/all_to_all | solution.py:46
  285.0 4.3 %all-to-all-start.5 = ((bf16[4,306,512]{2,1,0:T(8,128)(2,1)}), bf16[4,306,512]{2,1,0:T(8,128)(2,1)}, u32[]{:S(2)}, u32[]{:S(2)}) async-start(bf16[4,306,512]{2,1,0:T(8,128)(2,1)} %fusion.35), calls=%async_computation.6 | async-start | bytes 2555904 | tf_op jit(solution)/shard_map/all_to_all | solution.py:46
  290.2 5.1 %collective-permute-start.5 = (bf16[576,512]{1,0:T(8,128)(2,1)}, bf16[576,512]{1,0:T(8,128)(2,1)}, u32[]{:S(2)}, u32[]{:S(2)}) collective-permute-start(bf16[576,512]{1,0:T(8,128)(2,1)} %reduce-precision_convert_fusion.5), channel_id=1, source_target_pairs={{0,1},{3,2},{4,5},{7,6},{8,9},{11,10},{12,13},{15,14},{16,17},{19,... | collective-permute-start | bytes 1769480 | tf_op jit(solution)/shard_map/ppermute | solution.py:55
  295.3 2.7 convert_reduce_fusion
  300.2 2.2 collective-permute-start.9
  302.4 1.8 fusion.66
  306.9 1.7 copy.313
  308.6 2.0 all-to-all-done.5
  310.7 4.9 %all-to-all-start.4 = ((bf16[2,12,12,256]{3,0,2,1:T(2,128)(2,1)}), bf16[2,12,12,256]{3,0,2,1:T(2,128)(2,1)}, u32[]{:S(2)}, u32[]{:S(2)}) async-start(bf16[2,12,12,256]{3,0,2,1:T(2,128)(2,1)} %copy.313), calls=%async_computation.4 | async-start | bytes 294912 | tf_op jit(solution)/shard_map/all_to_all | solution.py:26
  315.5 1.7 convert_reduce_fusion.2
  318.1 4.7 %collective-permute-start.1 = (bf16[306,512]{1,0:T(8,128)(2,1)}, bf16[306,512]{1,0:T(8,128)(2,1)}, u32[]{:S(2)}, u32[]{:S(2)}) collective-permute-start(bf16[306,512]{1,0:T(8,128)(2,1)} %reduce-precision_convert_fusion.8), channel_id=1, source_target_pairs={{0,1},{3,2},{4,5},{7,6},{8,9},{11,10},{12,13},{15,14},{16,17},{19,... | collective-permute-start | bytes 940040 | tf_op jit(solution)/shard_map/ppermute | solution.py:55
  322.8 2.1 reduce-precision_convert_fusion.4
  326.6 2.4 reduce-precision_convert_fusion.1
  330.6 5.6 %all-to-all-start.1 = ((bf16[2,12,12,512]{3,0,2,1:T(2,128)(2,1)}), bf16[2,12,12,512]{3,0,2,1:T(2,128)(2,1)}, u32[]{:S(2)}, u32[]{:S(2)}) async-start(bf16[2,12,12,512]{3,0,2,1:T(2,128)(2,1)} %copy.298), calls=%async_computation.1 | async-start | bytes 589824 | tf_op jit(solution)/shard_map/all_to_all | solution.py:26
  340.0 26.8 %all-to-all-done.1 = bf16[2,12,12,512]{3,0,2,1:T(2,128)(2,1)} async-done(((bf16[2,12,12,512]{3,0,2,1:T(2,128)(2,1)}), bf16[2,12,12,512]{3,0,2,1:T(2,128)(2,1)}, u32[]{:S(2)}, u32[]{:S(2)}) %all-to-all-start.1) | async-done | bytes 294944 | tf_op jit(solution)/shard_map/all_to_all | solution.py:26
  370.2 2.2 reduce-precision_convert_fusion.3
  376.6 5.6 %collective-permute-done.3 = bf16[306,512]{1,0:T(8,128)(2,1)S(1)} collective-permute-done((bf16[306,512]{1,0:T(8,128)(2,1)S(1)}, bf16[306,512]{1,0:T(8,128)(2,1)S(1)}, u32[]{:S(2)}, u32[]{:S(2)}) %collective-permute-start.3) | collective-permute-done | bytes 313376 | tf_op jit(solution)/shard_map/ppermute | solution.py:61
  386.5 1.8 convert_element_type.320
  388.3 6.7 %collective-permute-done.7 = bf16[576,512]{1,0:T(8,128)(2,1)} collective-permute-done((bf16[576,512]{1,0:T(8,128)(2,1)}, bf16[576,512]{1,0:T(8,128)(2,1)}, u32[]{:S(2)}, u32[]{:S(2)}) %collective-permute-start.7) | collective-permute-done | bytes 589856 | tf_op jit(solution)/shard_map/ppermute | solution.py:61
  397.3 13.7 %collective-permute-done.11 = bf16[832,512]{1,0:T(8,128)(2,1)} collective-permute-done((bf16[832,512]{1,0:T(8,128)(2,1)S(1)}, bf16[832,512]{1,0:T(8,128)(2,1)}, u32[]{:S(2)}, u32[]{:S(2)}) %collective-permute-start.11) | collective-permute-done | bytes 852000 | tf_op jit(solution)/shard_map/ppermute | solution.py:61
  (368 shorter events, 99.9 us)
Async XLA Ops:
  7.2 57.2 %copy-start = (bf16[9,256,512]{2,1,0:T(8,128)(2,1)S(1)}, bf16[9,256,512]{2,1,0:T(8,128)(2,1)}, u32[]{:S(2)}) copy-start(bf16[9,256,512]{2,1,0:T(8,128)(2,1)} %param.30) | copy-start | bytes 7077892
  9.2 30.0 %all-to-all-start.2 = ((bf16[8,3,12,512]{3,2,1,0:T(8,128)(2,1)}), bf16[8,3,12,512]{3,2,1,0:T(8,128)(2,1)S(1)}, u32[]{:S(2)}, u32[]{:S(2)}) async-start(bf16[8,3,12,512]{3,2,1,0:T(8,128)(2,1)} %copy.300), calls=%async_computation.2 | async-start | bytes 786432 | tf_op jit(solution)/shard_map/all_to_all | solution.py:22
  33.4 5.7 %copy-start.55 = (s32[1152]{0:T(1024)}, s32[1152]{0:T(1024)S(1)}, u32[]{:S(2)}) copy-start(s32[1152]{0:T(1024)S(1)} %sub.164) | copy-start | bytes 13828
  39.1 17.4 %copy-start.38 = (bf16[8,3,12,256]{3,0,2,1:T(8,128)(2,1)S(1)}, bf16[8,3,12,256]{3,0,2,1:T(8,128)(2,1)}, u32[]{:S(2)}) copy-start(bf16[8,3,12,256]{3,0,2,1:T(8,128)(2,1)} %param.25) | copy-start | bytes 442372
  39.1 24.5 %copy-start.31 = (bf16[256,256]{1,0:T(8,128)(2,1)S(1)}, bf16[256,256]{1,0:T(8,128)(2,1)}, u32[]{:S(2)}) copy-start(bf16[256,256]{1,0:T(8,128)(2,1)} %param.28) | copy-start | bytes 393220
  39.1 24.5 %copy-start.63 = (f32[256]{0:T(256)S(1)}, f32[256]{0:T(256)}, u32[]{:S(2)}) copy-start(f32[256]{0:T(256)} %param.29) | copy-start | bytes 3076
  39.2 17.3 %all-to-all-start = ((bf16[4,288,256]{2,1,0:T(8,128)(2,1)}), bf16[4,288,256]{2,1,0:T(8,128)(2,1)}, u32[]{:S(2)}, u32[]{:S(2)}) async-start(bf16[4,288,256]{2,1,0:T(8,128)(2,1)} %bitcast), calls=%async_computation | async-start | bytes 1179648 | tf_op jit(solution)/shard_map/all_to_all | solution.py:173
  44.0 20.1 %copy-start.19 = (bf16[2,4,3,12,512]{4,0,3,2,1:T(2,128)(2,1)}, bf16[2,4,3,12,512]{4,0,3,2,1:T(2,128)(2,1)S(1)}, u32[]{:S(2)}) copy-start(bf16[2,4,3,12,512]{4,0,3,2,1:T(2,128)(2,1)S(1)} %copy.304) | copy-start | bytes 884740
  48.0 16.4 %copy-start.64 = (f32[512]{0:T(512)S(1)}, f32[512]{0:T(512)}, u32[]{:S(2)}) copy-start(f32[512]{0:T(512)} %param.31) | copy-start | bytes 6148
  57.4 136.9 %all-to-all-start.3 = ((bf16[4,8,3,12,256]{4,1,3,2,0:T(8,128)(2,1)}), bf16[4,8,3,12,256]{4,1,3,2,0:T(8,128)(2,1)}, u32[]{:S(2)}, u32[]{:S(2)}) async-start(bf16[4,8,3,12,256]{4,1,3,2,0:T(8,128)(2,1)} %broadcast_in_dim.2), calls=%async_computation.3 | async-start | bytes 1179648 | tf_op jit(solution)/shard_map/all_to_all | solution.py:32
  68.0 5.7 %copy-start.14 = (bf16[2,12,12,9,512]{4,2,1,0,3:T(8,128)(2,1)}, bf16[2,12,12,9,512]{4,2,1,0,3:T(8,128)(2,1)S(1)}, u32[]{:S(2)}) copy-start(bf16[2,12,12,9,512]{4,2,1,0,3:T(8,128)(2,1)S(1)} %bitcast_dynamic-update-slice_fusion.36) | copy-start | bytes 7962628
  68.0 5.7 %copy-start.43 = (f32[512]{0:T(512)S(1)}, f32[512]{0:T(512)}, u32[]{:S(2)}) copy-start(f32[512]{0:T(512)} %param.35) | copy-start | bytes 6148
  68.0 6.6 %copy-start.49 = (f32[512]{0:T(512)S(1)}, f32[512]{0:T(512)}, u32[]{:S(2)}) copy-start(f32[512]{0:T(512)} %param.36) | copy-start | bytes 6148
  68.0 6.6 %copy-start.51 = (f32[512]{0:T(512)S(1)}, f32[512]{0:T(512)}, u32[]{:S(2)}) copy-start(f32[512]{0:T(512)} %param.37) | copy-start | bytes 6148
  76.1 5.7 %copy-start.15 = (bf16[2,12,12,9,512]{4,2,1,0,3:T(8,128)(2,1)}, bf16[2,12,12,9,512]{4,2,1,0,3:T(8,128)(2,1)S(1)}, u32[]{:S(2)}) copy-start(bf16[2,12,12,9,512]{4,2,1,0,3:T(8,128)(2,1)S(1)} %bitcast_dynamic-update-slice_fusion.27) | copy-start | bytes 7962628
  76.1 5.7 %copy-start.4 = (f32[2,12,12,512]{3,2,1,0:T(8,128)S(1)}, f32[2,12,12,512]{3,2,1,0:T(8,128)}, u32[]{:S(2)}) copy-start(f32[2,12,12,512]{3,2,1,0:T(8,128)} %copy-done.3) | copy-start | bytes 1769476
  76.1 5.7 %copy-start.62 = (f32[512]{0:T(512)S(1)}, f32[512]{0:T(512)}, u32[]{:S(2)}) copy-start(f32[512]{0:T(512)} %param.39) | copy-start | bytes 6148
  82.0 22.6 %copy-start.1 = (f32[2,12,12,512]{3,2,1,0:T(8,128)}, f32[2,12,12,512]{3,2,1,0:T(8,128)S(1)}, u32[]{:S(2)}) copy-start(f32[2,12,12,512]{3,2,1,0:T(8,128)S(1)} %get-tuple-element.45) | copy-start | bytes 1769476
  83.7 4.9 %copy-start.66 = (f32[512]{0:T(512)S(1)}, f32[512]{0:T(512)}, u32[]{:S(2)}) copy-start(f32[512]{0:T(512)} %param.46) | copy-start | bytes 6148
  84.2 4.4 %copy-start.34 = (bf16[512,512]{1,0:T(8,128)(2,1)S(1)}, bf16[512,512]{1,0:T(8,128)(2,1)}, u32[]{:S(2)}) copy-start(bf16[512,512]{1,0:T(8,128)(2,1)} %param.45) | copy-start | bytes 1572868
  84.6 5.7 %copy-start.17 = (bf16[2,12,12,512]{3,0,2,1:T(2,128)(2,1)}, bf16[2,12,12,512]{3,0,2,1:T(2,128)(2,1)S(1)}, u32[]{:S(2)}) copy-start(bf16[2,12,12,512]{3,0,2,1:T(2,128)(2,1)S(1)} %copy.291) | copy-start | bytes 884740
  107.7 4.5 %copy-start.7 = (f32[2,12,12,512,1]{3,2,0,1,4:T(8,128)S(1)}, f32[2,12,12,512,1]{3,2,0,1,4:T(8,128)}, u32[]{:S(2)}) copy-start(f32[2,12,12,512,1]{3,2,0,1,4:T(8,128)} %copy-done.6) | copy-start | bytes 1769476
  107.7 4.5 %copy-start.42 = (f32[2,512]{1,0:T(2,128)S(1)}, f32[2,512]{1,0:T(2,128)}, u32[]{:S(2)}) copy-start(f32[2,512]{1,0:T(2,128)} %copy-done.41) | copy-start | bytes 12292
  107.7 4.5 %copy-start.44 = (f32[512]{0:T(512)S(1)}, f32[512]{0:T(512)}, u32[]{:S(2)}) copy-start(f32[512]{0:T(512)} %param.35) | copy-start | bytes 6148
  107.7 4.5 %copy-start.50 = (f32[512]{0:T(512)S(1)}, f32[512]{0:T(512)}, u32[]{:S(2)}) copy-start(f32[512]{0:T(512)} %param.36) | copy-start | bytes 6148
  107.7 4.5 %copy-start.52 = (f32[512]{0:T(512)S(1)}, f32[512]{0:T(512)}, u32[]{:S(2)}) copy-start(f32[512]{0:T(512)} %param.37) | copy-start | bytes 6148
  118.1 4.5 %copy-start.5 = (f32[2,12,12,512]{3,2,1,0:T(8,128)S(1)}, f32[2,12,12,512]{3,2,1,0:T(8,128)}, u32[]{:S(2)}) copy-start(f32[2,12,12,512]{3,2,1,0:T(8,128)} %copy-done.3) | copy-start | bytes 1769476
  118.1 4.5 %copy-start.40 = (f32[2,512]{1,0:T(2,128)S(1)}, f32[2,512]{1,0:T(2,128)}, u32[]{:S(2)}) copy-start(f32[2,512]{1,0:T(2,128)} %copy-done.39) | copy-start | bytes 12292
  118.2 4.5 %copy-start.48 = (f32[512]{0:T(512)S(1)}, f32[512]{0:T(512)}, u32[]{:S(2)}) copy-start(f32[512]{0:T(512)} %param.32) | copy-start | bytes 6148
  118.2 4.5 %copy-start.54 = (f32[512]{0:T(512)S(1)}, f32[512]{0:T(512)}, u32[]{:S(2)}) copy-start(f32[512]{0:T(512)} %param.33) | copy-start | bytes 6148
  142.0 5.8 %copy-start.18 = (bf16[2,12,12,512]{3,0,2,1:T(2,128)(2,1)S(1)}, bf16[2,12,12,512]{3,0,2,1:T(2,128)(2,1)}, u32[]{:S(2)}) copy-start(bf16[2,12,12,512]{3,0,2,1:T(2,128)(2,1)} %copy-done.17) | copy-start | bytes 884740
  144.0 7.1 %copy-start.20 = (bf16[2,4,3,12,512]{4,0,3,2,1:T(2,128)(2,1)S(1)}, bf16[2,4,3,12,512]{4,0,3,2,1:T(2,128)(2,1)}, u32[]{:S(2)}) copy-start(bf16[2,4,3,12,512]{4,0,3,2,1:T(2,128)(2,1)} %copy-done.19) | copy-start | bytes 884740
  145.6 44.2 %collective-permute-start.4 = (bf16[4,576,512]{2,1,0:T(8,128)(2,1)}, bf16[4,576,512]{2,1,0:T(8,128)(2,1)}, u32[]{:S(2)}, u32[]{:S(2)}) collective-permute-start(bf16[4,576,512]{2,1,0:T(8,128)(2,1)} %dynamic-slice_bitcast_fusion.1), channel_id=1, source_target_pairs={{0,4},{4,0},{8,12},{12,8},{16,20},{20,16},{24,28},{28,24},{1,5},{5... | collective-permute-start | bytes 7077896 | tf_op jit(solution)/shard_map/ppermute | solution.py:43
  149.0 7.0 %copy-start.30 = (bf16[2,144,512]{2,1,0:T(8,128)(2,1)S(1)}, bf16[2,144,512]{2,1,0:T(8,128)(2,1)}, u32[]{:S(2)}) copy-start(bf16[2,144,512]{2,1,0:T(8,128)(2,1)} %fusion.63) | copy-start | bytes 884740
  151.1 7.2 %copy-start.33 = (bf16[4,2,64,2,144]{4,2,3,1,0:T(8,128)(2,1)S(1)}, bf16[4,2,64,2,144]{4,2,3,1,0:T(8,128)(2,1)}, u32[]{:S(2)}) copy-start(bf16[4,2,64,2,144]{4,2,3,1,0:T(8,128)(2,1)} %copy.327) | copy-start | bytes 884740
  151.1 7.2 %copy-start.37 = (bf16[2,144,512]{2,1,0:T(8,128)(2,1)S(1)}, bf16[2,144,512]{2,1,0:T(8,128)(2,1)}, u32[]{:S(2)}) copy-start(bf16[2,144,512]{2,1,0:T(8,128)(2,1)} %get-tuple-element.74) | copy-start | bytes 884740
  177.6 4.5 %copy-start.58 = (f32[2,32]{1,0:T(2,128)S(1)}, f32[2,32]{1,0:T(2,128)}, u32[]{:S(2)}) copy-start(f32[2,32]{1,0:T(2,128)} %reduce_sum.404) | copy-start | bytes 772
  177.6 4.5 %copy-start.59 = (f32[2,32]{1,0:T(2,128)S(1)}, f32[2,32]{1,0:T(2,128)}, u32[]{:S(2)}) copy-start(f32[2,32]{1,0:T(2,128)} %reduce_sum.401) | copy-start | bytes 772
  177.6 6.0 %copy-start.2 = (f32[2,12,12,512]{3,2,1,0:T(8,128)S(1)}, f32[2,12,12,512]{3,2,1,0:T(8,128)}, u32[]{:S(2)}) copy-start(f32[2,12,12,512]{3,2,1,0:T(8,128)} %copy-done.1) | copy-start | bytes 1769476
  181.6 53.5 %collective-permute-start.8 = (bf16[4,832,512]{2,1,0:T(8,128)(2,1)}, bf16[4,832,512]{2,1,0:T(8,128)(2,1)}, u32[]{:S(2)}, u32[]{:S(2)}) collective-permute-start(bf16[4,832,512]{2,1,0:T(8,128)(2,1)} %dynamic-slice_bitcast_fusion), channel_id=1, source_target_pairs={{0,4},{4,0},{8,12},{12,8},{16,20},{20,16},{24,28},{28,24},{1,5},{5... | collective-permute-start | bytes 10223624 | tf_op jit(solution)/shard_map/ppermute | solution.py:43
  194.3 46.6 %all-to-all-start.6 = ((bf16[4,576,512]{2,1,0:T(8,128)(2,1)}), bf16[4,576,512]{2,1,0:T(8,128)(2,1)}, u32[]{:S(2)}, u32[]{:S(2)}) async-start(bf16[4,576,512]{2,1,0:T(8,128)(2,1)} %fusion.15), calls=%async_computation.7 | async-start | bytes 4718592 | tf_op jit(solution)/shard_map/all_to_all | solution.py:46
  204.6 21.1 %copy-start.57 = (bf16[8,64]{1,0:T(8,128)(2,1)S(1)}, bf16[8,64]{1,0:T(8,128)(2,1)}, u32[]{:S(2)}) copy-start(bf16[8,64]{1,0:T(8,128)(2,1)} %reshape.364) | copy-start | bytes 3076
  240.9 44.1 %all-to-all-start.7 = ((bf16[4,832,512]{2,1,0:T(8,128)(2,1)}), bf16[4,832,512]{2,1,0:T(8,128)(2,1)}, u32[]{:S(2)}, u32[]{:S(2)}) async-start(bf16[4,832,512]{2,1,0:T(8,128)(2,1)} %fusion.11), calls=%async_computation.8 | async-start | bytes 6815744 | tf_op jit(solution)/shard_map/all_to_all | solution.py:46
  245.6 140.9 %reduce-scatter.2.cloned.1.call-start = ((), (), s32[]{:S(2)}) async-start(), calls=%async_computation.9 | async-start | bytes 2359296 | tf_op jit(solution)/shard_map/reduce_scatter | solution.py:181
  256.1 10.1 %collective-permute-start = (bf16[4,306,512]{2,0,1:T(4,128)(2,1)}, bf16[4,306,512]{2,0,1:T(4,128)(2,1)}, u32[]{:S(2)}, u32[]{:S(2)}) collective-permute-start(bf16[4,306,512]{2,0,1:T(4,128)(2,1)} %copy.319), channel_id=1, source_target_pairs={{0,4},{4,0},{8,12},{12,8},{16,20},{20,16},{24,28},{28,24},{1,5},{5... | collective-permute-start | bytes 3760136 | tf_op jit(solution)/shard_map/ppermute | solution.py:43
  285.0 25.6 %all-to-all-start.5 = ((bf16[4,306,512]{2,1,0:T(8,128)(2,1)}), bf16[4,306,512]{2,1,0:T(8,128)(2,1)}, u32[]{:S(2)}, u32[]{:S(2)}) async-start(bf16[4,306,512]{2,1,0:T(8,128)(2,1)} %fusion.35), calls=%async_computation.6 | async-start | bytes 2555904 | tf_op jit(solution)/shard_map/all_to_all | solution.py:46
  290.2 12.2 %copy-start.23 = (bf16[288,256]{1,0:T(8,128)(2,1)S(1)}, bf16[288,256]{1,0:T(8,128)(2,1)}, u32[]{:S(2)}) copy-start(bf16[288,256]{1,0:T(8,128)(2,1)} %copy-done.22) | copy-start | bytes 442372
  290.2 12.2 %copy-start.28 = (bf16[288,256]{1,0:T(8,128)(2,1)S(1)}, bf16[288,256]{1,0:T(8,128)(2,1)}, u32[]{:S(2)}) copy-start(bf16[288,256]{1,0:T(8,128)(2,1)} %reshape.351) | copy-start | bytes 442372
  290.2 12.2 %copy-start.32 = (bf16[256,256]{1,0:T(8,128)(2,1)S(1)}, bf16[256,256]{1,0:T(8,128)(2,1)}, u32[]{:S(2)}) copy-start(bf16[256,256]{1,0:T(8,128)(2,1)} %param.28) | copy-start | bytes 393220
  290.2 14.0 %copy-start.27 = (bf16[2,12,12,512]{3,2,1,0:T(8,128)(2,1)S(1)}, bf16[2,12,12,512]{3,2,1,0:T(8,128)(2,1)}, u32[]{:S(2)}) copy-start(bf16[2,12,12,512]{3,2,1,0:T(8,128)(2,1)} %get-tuple-element.51) | copy-start | bytes 884740
  290.2 32.5 %collective-permute-start.5 = (bf16[576,512]{1,0:T(8,128)(2,1)}, bf16[576,512]{1,0:T(8,128)(2,1)}, u32[]{:S(2)}, u32[]{:S(2)}) collective-permute-start(bf16[576,512]{1,0:T(8,128)(2,1)} %reduce-precision_convert_fusion.5), channel_id=1, source_target_pairs={{0,1},{3,2},{4,5},{7,6},{8,9},{11,10},{12,13},{15,14},{16,17},{19,... | collective-permute-start | bytes 1769480 | tf_op jit(solution)/shard_map/ppermute | solution.py:55
  300.2 26.4 %collective-permute-start.9 = (bf16[832,512]{1,0:T(8,128)(2,1)}, bf16[832,512]{1,0:T(8,128)(2,1)}, u32[]{:S(2)}, u32[]{:S(2)}) collective-permute-start(bf16[832,512]{1,0:T(8,128)(2,1)} %reduce-precision_convert_fusion.2), channel_id=1, source_target_pairs={{0,1},{3,2},{4,5},{7,6},{8,9},{11,10},{12,13},{15,14},{16,17},{19,... | collective-permute-start | bytes 2555912 | tf_op jit(solution)/shard_map/ppermute | solution.py:55
  310.7 19.9 %all-to-all-start.4 = ((bf16[2,12,12,256]{3,0,2,1:T(2,128)(2,1)}), bf16[2,12,12,256]{3,0,2,1:T(2,128)(2,1)}, u32[]{:S(2)}, u32[]{:S(2)}) async-start(bf16[2,12,12,256]{3,0,2,1:T(2,128)(2,1)} %copy.313), calls=%async_computation.4 | async-start | bytes 294912 | tf_op jit(solution)/shard_map/all_to_all | solution.py:26
  315.5 11.1 %copy-start.10 = (f32[832,512]{1,0:T(8,128)S(1)}, f32[832,512]{1,0:T(8,128)}, u32[]{:S(2)}) copy-start(f32[832,512]{1,0:T(8,128)} %copy-done.9) | copy-start | bytes 5111812
  317.2 7.6 %copy-start.12 = (f32[306,512]{1,0:T(8,128)}, f32[306,512]{1,0:T(8,128)S(1)}, u32[]{:S(2)}) copy-start(f32[306,512]{1,0:T(8,128)S(1)} %convert_reduce_fusion.2) | copy-start | bytes 1880068
  318.1 18.1 %collective-permute-start.1 = (bf16[306,512]{1,0:T(8,128)(2,1)}, bf16[306,512]{1,0:T(8,128)(2,1)}, u32[]{:S(2)}, u32[]{:S(2)}) collective-permute-start(bf16[306,512]{1,0:T(8,128)(2,1)} %reduce-precision_convert_fusion.8), channel_id=1, source_target_pairs={{0,1},{3,2},{4,5},{7,6},{8,9},{11,10},{12,13},{15,14},{16,17},{19,... | collective-permute-start | bytes 940040 | tf_op jit(solution)/shard_map/ppermute | solution.py:55
  324.8 45.3 %collective-permute-start.6 = (bf16[576,512]{1,0:T(8,128)(2,1)}, bf16[576,512]{1,0:T(8,128)(2,1)}, u32[]{:S(2)}, u32[]{:S(2)}) collective-permute-start(bf16[576,512]{1,0:T(8,128)(2,1)} %reduce-precision_convert_fusion.4), channel_id=1, source_target_pairs={{1,2},{2,1},{5,6},{6,5},{9,10},{10,9},{13,14},{14,13},{17,18},{18,... | collective-permute-start | bytes 1769480 | tf_op jit(solution)/shard_map/ppermute | solution.py:58
  326.3 9.9 %copy-start.13 = (f32[306,512]{1,0:T(8,128)S(1)}, f32[306,512]{1,0:T(8,128)}, u32[]{:S(2)}) copy-start(f32[306,512]{1,0:T(8,128)} %copy-done.12) | copy-start | bytes 1880068
  329.0 44.7 %collective-permute-start.10 = (bf16[832,512]{1,0:T(8,128)(2,1)}, bf16[832,512]{1,0:T(8,128)(2,1)}, u32[]{:S(2)}, u32[]{:S(2)}) collective-permute-start(bf16[832,512]{1,0:T(8,128)(2,1)} %reduce-precision_convert_fusion.1), channel_id=1, source_target_pairs={{1,2},{2,1},{5,6},{6,5},{9,10},{10,9},{13,14},{14,13},{17,18},{18,... | collective-permute-start | bytes 2555912 | tf_op jit(solution)/shard_map/ppermute | solution.py:58
  330.6 36.2 %all-to-all-start.1 = ((bf16[2,12,12,512]{3,0,2,1:T(2,128)(2,1)}), bf16[2,12,12,512]{3,0,2,1:T(2,128)(2,1)}, u32[]{:S(2)}, u32[]{:S(2)}) async-start(bf16[2,12,12,512]{3,0,2,1:T(2,128)(2,1)} %copy.298), calls=%async_computation.1 | async-start | bytes 589824 | tf_op jit(solution)/shard_map/all_to_all | solution.py:26
  337.2 31.5 %collective-permute-start.2 = (bf16[306,512]{1,0:T(8,128)(2,1)S(1)}, bf16[306,512]{1,0:T(8,128)(2,1)S(1)}, u32[]{:S(2)}, u32[]{:S(2)}) collective-permute-start(bf16[306,512]{1,0:T(8,128)(2,1)S(1)} %reduce-precision_convert_fusion.7), channel_id=1, source_target_pairs={{1,2},{2,1},{5,6},{6,5},{9,10},{10,9},{13,14},{14,13},{17,18},{18,... | collective-permute-start | bytes 940040 | tf_op jit(solution)/shard_map/ppermute | solution.py:58
  368.8 13.4 %collective-permute-start.3 = (bf16[306,512]{1,0:T(8,128)(2,1)S(1)}, bf16[306,512]{1,0:T(8,128)(2,1)S(1)}, u32[]{:S(2)}, u32[]{:S(2)}) collective-permute-start(bf16[306,512]{1,0:T(8,128)(2,1)S(1)} %reduce-precision_convert_fusion.6), channel_id=1, source_target_pairs={{1,0},{2,3},{5,4},{6,7},{9,8},{10,11},{13,12},{14,15},{17,16},{18,... | collective-permute-start | bytes 940040 | tf_op jit(solution)/shard_map/ppermute | solution.py:61
  372.4 22.6 %collective-permute-start.7 = (bf16[576,512]{1,0:T(8,128)(2,1)}, bf16[576,512]{1,0:T(8,128)(2,1)}, u32[]{:S(2)}, u32[]{:S(2)}) collective-permute-start(bf16[576,512]{1,0:T(8,128)(2,1)} %reduce-precision_convert_fusion.3), channel_id=1, source_target_pairs={{1,0},{2,3},{5,4},{6,7},{9,8},{10,11},{13,12},{14,15},{17,16},{18,... | collective-permute-start | bytes 1769480 | tf_op jit(solution)/shard_map/ppermute | solution.py:61
  375.3 35.7 %collective-permute-start.11 = (bf16[832,512]{1,0:T(8,128)(2,1)S(1)}, bf16[832,512]{1,0:T(8,128)(2,1)}, u32[]{:S(2)}, u32[]{:S(2)}) collective-permute-start(bf16[832,512]{1,0:T(8,128)(2,1)S(1)} %reduce-precision_convert_fusion), channel_id=1, source_target_pairs={{1,0},{2,3},{5,4},{6,7},{9,8},{10,11},{13,12},{14,15},{17,16},{18,... | collective-permute-start | bytes 2555912 | tf_op jit(solution)/shard_map/ppermute | solution.py:61
  (25 other events, 49.7 us)
Sparse Core Ops, SparseCore 0:
  266.3 54.4 reduce-scatter.1
